TPU v7x, 128 devices: a whole 4x4x4 slice. The times are simulated.
128 devices in a mesh: dp: 2 (over core), seq: 16 (over y, z), tensor: 4 (over x).
Axes of the slice: x: 4, y: 4, z: 4, core: 2. Of those that a mesh axis runs over, the one named last changes fastest.
Arguments:
- block_input: bfloat16 [2, 4096, 1024], P('dp', 'seq'), may hold values from -6 to 6
- upstream_grad: bfloat16 [2, 4096, 1024], P('dp', 'seq'), may hold values from -6 to 6
- query_weight: float32 [1024, 1024], P(('dp', 'seq'), 'tensor'), may hold values from -0.1875 to 0.1875
- key_value_weight: float32 [1024, 2, 512], P(('dp', 'seq'), None, 'tensor'), may hold values from -0.1875 to 0.1875
- output_weight: float32 [1024, 1024], P(('dp', 'seq'), 'tensor'), may hold values from -4 to 4
- gateup_weight: float32 [1024, 2, 4608], P(('dp', 'seq'), None, 'tensor'), may hold values from -0.1875 to 0.1875
- down_weight: float32 [1024, 4608], P(('dp', 'seq'), 'tensor'), may hold values from -0.09375 to 0.09375
- norm_gains: float32 [1024, 2], P(('dp', 'seq')), may hold values from 0.5 to 1.5
- head_norm_gains: float32 [2, 64], replicated, may hold values from 0.6 to 1.6
- query_momentum: float32 [1024, 1024], P(('dp', 'seq'), 'tensor'), may hold values from -5.43058 to 5.43058
- query_variance: float32 [1024, 1024], P(('dp', 'seq'), 'tensor'), may hold values from 1556.48 to 6225.92
- key_value_momentum: float32 [1024, 2, 512], P(('dp', 'seq'), None, 'tensor'), may hold values from -5.43058 to 5.43058
- key_value_variance: float32 [1024, 2, 512], P(('dp', 'seq'), None, 'tensor'), may hold values from 1556.48 to 6225.92
- output_momentum: float32 [1024, 1024], P(('dp', 'seq'), 'tensor'), may hold values from -10.86116 to 10.86116
- output_variance: float32 [1024, 1024], P(('dp', 'seq'), 'tensor'), may hold values from 12.288 to 49.152
- gateup_momentum: float32 [1024, 2, 4608], P(('dp', 'seq'), None, 'tensor'), may hold values from -13.57645 to 13.57645
- gateup_variance: float32 [1024, 2, 4608], P(('dp', 'seq'), None, 'tensor'), may hold values from 81.92 to 327.68
- down_momentum: float32 [1024, 4608], P(('dp', 'seq'), 'tensor'), may hold values from -32.58348 to 32.58348
- down_variance: float32 [1024, 4608], P(('dp', 'seq'), 'tensor'), may hold values from 491.52 to 1966.08
- norm_momentum: float32 [1024, 2], P(('dp', 'seq')), may hold values from -54.3058 to 54.3058
- norm_variance: float32 [1024, 2], P(('dp', 'seq')), may hold values from 9830.4 to 39321.6
- head_momentum: float32 [2, 64], replicated, may hold values from -86.88928 to 86.88928
- head_variance: float32 [2, 64], replicated, may hold values from 39321 to 157286
Outputs:
- block_output: bfloat16 [2, 4096, 1024], P('dp', 'seq')
- input_grad: float32 [2, 4096, 1024], P('dp', 'seq')
- query_grad: float32 [1024, 1024], P(('dp', 'seq'), 'tensor')
- keyvalue_grad: float32 [1024, 2, 512], P(('dp', 'seq'), None, 'tensor')
- output_grad: float32 [1024, 1024], P(('dp', 'seq'), 'tensor')
- gateup_grad: float32 [1024, 2, 4608], P(('dp', 'seq'), None, 'tensor')
- down_grad: float32 [1024, 4608], P(('dp', 'seq'), 'tensor')
- norm_grad: float32 [1024, 2], P(('dp', 'seq'))
- head_grad: float32 [2, 64], replicated
- query_direction: float32 [1024, 1024], P(('dp', 'seq'), 'tensor')
- keyvalue_direction: float32 [1024, 2, 512], P(('dp', 'seq'), None, 'tensor')
- output_direction: float32 [1024, 1024], P(('dp', 'seq'), 'tensor')
- gateup_direction: float32 [1024, 2, 4608], P(('dp', 'seq'), None, 'tensor')
- down_direction: float32 [1024, 4608], P(('dp', 'seq'), 'tensor')
- norm_direction: float32 [1024, 2], P(('dp', 'seq'))
- head_direction: float32 [2, 64], replicated
- query_first: float32 [1024, 1024], P(('dp', 'seq'), 'tensor')
- query_second: float32 [1024, 1024], P(('dp', 'seq'), 'tensor')
- keyvalue_first: float32 [1024, 2, 512], P(('dp', 'seq'), None, 'tensor')
- keyvalue_second: float32 [1024, 2, 512], P(('dp', 'seq'), None, 'tensor')
- output_first: float32 [1024, 1024], P(('dp', 'seq'), 'tensor')
- output_second: float32 [1024, 1024], P(('dp', 'seq'), 'tensor')
- gateup_first: float32 [1024, 2, 4608], P(('dp', 'seq'), None, 'tensor')
- gateup_second: float32 [1024, 2, 4608], P(('dp', 'seq'), None, 'tensor')
- down_first: float32 [1024, 4608], P(('dp', 'seq'), 'tensor')
- down_second: float32 [1024, 4608], P(('dp', 'seq'), 'tensor')
- norm_first: float32 [1024, 2], P(('dp', 'seq'))
- norm_second: float32 [1024, 2], P(('dp', 'seq'))
- head_first: float32 [2, 64], replicated
- head_second: float32 [2, 64], replicated
All inputs are finite; a program needn't handle non-finite values.
Results may differ from a plain program's by a relative error of at most 0.025.
Values may be sent and summed in bfloat16 or wider, within the bound.
A program may use at most 128 MiB of HBM per device.

v0:
```python
import jax
import jax.numpy as jnp
from jax import lax
from jax.sharding import PartitionSpec as P

QUERY_HEADS = 16
KEY_VALUE_HEADS = 8
HEAD_SIZE = 64


norm_eps = 1e-05
rope_base = 1000000.0
beta_one = 0.9
beta_two = 0.95
adam_eps = 1e-08
decay_rate = 0.1
adam_count = 3
masked_score = -1e30


def as_sent(x):

    def short(part):
        return part.astype(jnp.bfloat16) if part.dtype == jnp.float32 else part

    return jax.tree.map(short, x)


def rms_forward(values, gain_row):
    inverse = lax.rsqrt(jnp.mean(values * values, axis=-1, keepdims=True) + norm_eps)
    normed = values * inverse
    return (normed * gain_row, normed, inverse)


def root_mean_square_backward(grad_out, gain_row, normed, inverse):
    grad_normed = grad_out * gain_row
    inner_mean = jnp.mean(grad_normed * normed, axis=-1, keepdims=True)
    return inverse * (grad_normed - normed * inner_mean)


def rope_tables(positions, head_width):
    half_width = head_width // 2
    frequency = rope_base ** (-(jnp.arange(half_width, dtype=jnp.float32) * 2.0) / head_width)
    angles = positions.astype(jnp.float32)[:, None] * frequency[None, :]
    return (jnp.cos(angles), jnp.sin(angles))


def rotate(values, cosine, sine_table):
    half_width = values.shape[-1] // 2
    first_half = values[..., :half_width]
    second_half = values[..., half_width:]
    cos_rows = cosine[:, None, :]
    sin_rows = sine_table[:, None, :]
    return jnp.concatenate(
        [
            first_half * cos_rows - second_half * sin_rows,
            second_half * cos_rows + first_half * sin_rows,
        ],
        axis=-1,
    )


def rotate_back(gradient, cosine, sine_table):
    half_width = gradient.shape[-1] // 2
    first_half = gradient[..., :half_width]
    second_half = gradient[..., half_width:]
    cos_rows = cosine[:, None, :]
    sin_rows = sine_table[:, None, :]
    return jnp.concatenate(
        [
            first_half * cos_rows + second_half * sin_rows,
            second_half * cos_rows - first_half * sin_rows,
        ],
        axis=-1,
    )


def contract_rows(left, right):
    return lax.dot_general(
        left, right, (((0,), (0,)), ((), ())), preferred_element_type=jnp.float32
    )


def contract_cols(left, right):
    return lax.dot_general(
        left, right, (((1,), (1,)), ((), ())), preferred_element_type=jnp.float32
    )


def group_rows(values, group_count):
    count, heads, head_width = values.shape
    return (
        values.reshape(count, heads // group_count, group_count, head_width)
        .transpose(1, 2, 0, 3)
        .reshape(heads // group_count, group_count * count, head_width)
    )


def ungroup_rows(values, group_count):
    kv_heads, rows, head_width = values.shape
    count = rows // group_count
    return (
        values.reshape(kv_heads, group_count, count, head_width)
        .transpose(2, 0, 1, 3)
        .reshape(count, kv_heads * group_count, head_width)
    )


def attend_forward(query_rows, keys_all, values_all, row_pos):
    kv_heads, rows, head_width = query_rows.shape
    sequence_length = keys_all.shape[0]
    rows_per_block = 512
    factor = 1.0 / head_width**0.5
    key_blocks = keys_all.reshape(
        sequence_length // rows_per_block, rows_per_block, kv_heads, head_width
    )
    value_blocks = values_all.reshape(
        sequence_length // rows_per_block, rows_per_block, kv_heads, head_width
    )
    last_row = jnp.max(row_pos)

    def visit(carried, block_input):
        key_blk, value_blk, block_index = block_input
        first_key = block_index * rows_per_block

        def active(state_in):
            running_max, running_sum, accumulated = state_in
            scores = (
                jnp.einsum("hrd,khd->hrk", query_rows, key_blk, preferred_element_type=jnp.float32)
                * factor
            )
            causal = (first_key + jnp.arange(rows_per_block, dtype=jnp.int32))[None, :] <= row_pos[
                :, None
            ]
            scores = jnp.where(causal[None], scores, masked_score)
            new_max = jnp.maximum(running_max, jnp.max(scores, axis=-1))
            shrink = jnp.exp(running_max - new_max)
            exp_scores = jnp.exp(scores - new_max[..., None])
            new_sum = running_sum * shrink + jnp.sum(exp_scores, axis=-1)
            accumulated = accumulated * shrink[..., None] + jnp.einsum(
                "hrk,khd->hrd",
                exp_scores.astype(jnp.bfloat16),
                value_blk,
                preferred_element_type=jnp.float32,
            )
            return (new_max, new_sum, accumulated)

        def passed(state_in):
            return state_in

        return (lax.cond(first_key <= last_row, active, passed, carried), None)

    initial = (
        jnp.full((kv_heads, rows), masked_score, jnp.float32),
        jnp.zeros((kv_heads, rows), jnp.float32),
        jnp.zeros((kv_heads, rows, head_width), jnp.float32),
    )
    (running_max, running_sum, accumulated), unused = lax.scan(
        visit,
        initial,
        (key_blocks, value_blocks, jnp.arange(sequence_length // rows_per_block, dtype=jnp.int32)),
    )
    output = (accumulated / running_sum[..., None]).astype(jnp.bfloat16)
    return (output, running_max + jnp.log(running_sum))


def attend_backward(query_rows, keys_all, values_all, out_rows, log_total, grad_rows, row_pos):
    kv_heads, rows, head_width = query_rows.shape
    sequence_length = keys_all.shape[0]
    rows_per_block = 512
    factor = 1.0 / head_width**0.5
    key_blocks = keys_all.reshape(
        sequence_length // rows_per_block, rows_per_block, kv_heads, head_width
    )
    value_blocks = values_all.reshape(
        sequence_length // rows_per_block, rows_per_block, kv_heads, head_width
    )
    last_row = jnp.max(row_pos)
    delta = jnp.sum(grad_rows.astype(jnp.float32) * out_rows.astype(jnp.float32), axis=-1)

    def visit(grad_query, block_input):
        key_blk, value_blk, block_index = block_input
        first_key = block_index * rows_per_block

        def active(grad_in):
            scores = (
                jnp.einsum("hrd,khd->hrk", query_rows, key_blk, preferred_element_type=jnp.float32)
                * factor
            )
            causal = (first_key + jnp.arange(rows_per_block, dtype=jnp.int32))[None, :] <= row_pos[
                :, None
            ]
            scores = jnp.where(causal[None], scores, masked_score)
            probs = jnp.where(causal[None], jnp.exp(scores - log_total[..., None]), 0.0)
            value_gradient = jnp.einsum(
                "hrk,hrd->khd",
                probs.astype(jnp.bfloat16),
                grad_rows,
                preferred_element_type=jnp.float32,
            )
            grad_probs = jnp.einsum(
                "hrd,khd->hrk", grad_rows, value_blk, preferred_element_type=jnp.float32
            )
            grad_scores = (probs * (grad_probs - delta[..., None])).astype(jnp.bfloat16)
            grad_out = grad_in + factor * jnp.einsum(
                "hrk,khd->hrd", grad_scores, key_blk, preferred_element_type=jnp.float32
            )
            key_gradient = factor * jnp.einsum(
                "hrk,hrd->khd", grad_scores, query_rows, preferred_element_type=jnp.float32
            )
            return (grad_out, (key_gradient, value_gradient))

        def passed(grad_in):
            nothing = jnp.zeros((rows_per_block, kv_heads, head_width), jnp.float32)
            return (grad_in, (nothing, nothing))

        return lax.cond(first_key <= last_row, active, passed, grad_query)

    initial = jnp.zeros((kv_heads, rows, head_width), jnp.float32)
    grad_query, (grad_keys, grad_values) = lax.scan(
        visit,
        initial,
        (key_blocks, value_blocks, jnp.arange(sequence_length // rows_per_block, dtype=jnp.int32)),
    )
    return (
        grad_query,
        grad_keys.reshape(sequence_length, kv_heads * head_width),
        grad_values.reshape(sequence_length, kv_heads * head_width),
    )


def adamw(weight, momentum, variance, gradient, decay):
    first = beta_one * momentum + (1.0 - beta_one) * gradient
    second = beta_two * variance + (1.0 - beta_two) * gradient * gradient
    first_fixed = first / (1.0 - beta_one**adam_count)
    second_fixed = second / (1.0 - beta_two**adam_count)
    direction = first_fixed / (jnp.sqrt(second_fixed) + adam_eps) + decay * weight
    return (direction, first, second)


def forward_one(input16, weights, head_norm_gains, cosine, sine_table, row_pos):
    (
        query_matrix,
        key_value_matrix,
        output_matrix,
        gateup_matrix,
        down_matrix,
        gain_one,
        gain_two,
    ) = weights
    group_count = QUERY_HEADS // KEY_VALUE_HEADS
    count = input16.shape[0]
    heads_local = query_matrix.shape[1] // HEAD_SIZE
    kv_local = key_value_matrix.shape[2] // HEAD_SIZE
    resid_in = input16.astype(jnp.float32)
    first_norm, normed_one, inverse_one = rms_forward(resid_in, gain_one)
    hidden_first = first_norm.astype(jnp.bfloat16)
    query = jnp.dot(hidden_first, query_matrix, preferred_element_type=jnp.float32).reshape(
        count, heads_local, HEAD_SIZE
    )
    key_unnormed = jnp.dot(
        hidden_first, key_value_matrix[:, 0, :], preferred_element_type=jnp.float32
    ).reshape(count, kv_local, HEAD_SIZE)
    value_half16 = jnp.dot(
        hidden_first, key_value_matrix[:, 1, :], preferred_element_type=jnp.float32
    ).astype(jnp.bfloat16)
    query_norm, query_hat, query_inverse = rms_forward(query, head_norm_gains[0])
    key_norm, key_normalized, key_inverse_norm = rms_forward(key_unnormed, head_norm_gains[1])
    query_half16 = rotate(query_norm, cosine, sine_table).astype(jnp.bfloat16)
    key16 = (
        rotate(key_norm, cosine, sine_table)
        .astype(jnp.bfloat16)
        .reshape(count, kv_local * HEAD_SIZE)
    )
    keys_all, values_all = (
        lax.all_gather(key16, "seq", axis=0, tiled=True),
        lax.all_gather(value_half16, "seq", axis=0, tiled=True),
    )
    query_rows = group_rows(query_half16, group_count)
    out_rows, log_total = attend_forward(query_rows, keys_all, values_all, row_pos)
    out_flat = ungroup_rows(out_rows, group_count).reshape(count, heads_local * HEAD_SIZE)
    attn_sum = lax.psum(contract_cols(out_flat, output_matrix), "tensor")
    resid_mid = resid_in + attn_sum
    second_norm, normed_two, inverse_two = rms_forward(resid_mid, gain_two)
    hidden_two = second_norm.astype(jnp.bfloat16)
    gate = jnp.dot(hidden_two, gateup_matrix[:, 0, :], preferred_element_type=jnp.float32)
    upward = jnp.dot(hidden_two, gateup_matrix[:, 1, :], preferred_element_type=jnp.float32)
    sigmoid_gate = jax.nn.sigmoid(gate)
    silu_gate = gate * sigmoid_gate
    inner16 = (silu_gate * upward).astype(jnp.bfloat16)
    ffn_sum = lax.psum(contract_cols(inner16, down_matrix).astype(jnp.bfloat16), "tensor").astype(
        jnp.float32
    )
    output16 = (resid_mid + ffn_sum).astype(jnp.bfloat16)
    saved = (
        normed_one,
        inverse_one,
        hidden_first,
        query_hat,
        query_inverse,
        key_normalized,
        key_inverse_norm,
        query_rows,
        keys_all,
        values_all,
        out_rows,
        log_total,
        out_flat,
        normed_two,
        inverse_two,
        hidden_two,
        gate,
        upward,
        sigmoid_gate,
        silu_gate,
        inner16,
    )
    return (output16, saved)


def backward_one(upstream16, saved, weights, head_norm_gains, cosine, sine_table, row_pos):
    (
        query_matrix,
        key_value_matrix,
        output_matrix,
        gateup_matrix,
        down_matrix,
        gain_one,
        gain_two,
    ) = weights
    (
        normed_one,
        inverse_one,
        hidden_first,
        query_hat,
        query_inverse,
        key_normalized,
        key_inverse_norm,
        query_rows,
        keys_all,
        values_all,
        out_rows,
        log_total,
        out_flat,
        normed_two,
        inverse_two,
        hidden_two,
        gate,
        upward,
        sigmoid_gate,
        silu_gate,
        inner16,
    ) = saved
    group_count = QUERY_HEADS // KEY_VALUE_HEADS
    count = upstream16.shape[0]
    heads_local = query_matrix.shape[1] // HEAD_SIZE
    kv_local = key_value_matrix.shape[2] // HEAD_SIZE
    grad_down = contract_rows(upstream16, inner16)
    grad_inner = jnp.dot(upstream16, down_matrix, preferred_element_type=jnp.float32)
    grad_gate16 = (grad_inner * upward * sigmoid_gate * (1.0 + gate * (1.0 - sigmoid_gate))).astype(
        jnp.bfloat16
    )
    grad_up16 = (grad_inner * silu_gate).astype(jnp.bfloat16)
    grad_gateup = jnp.stack(
        [contract_rows(hidden_two, grad_gate16), contract_rows(hidden_two, grad_up16)], axis=1
    )
    hidden_two_part = contract_cols(grad_gate16, gateup_matrix[:, 0, :]) + contract_cols(
        grad_up16, gateup_matrix[:, 1, :]
    )
    grad_hidden_two = lax.psum(hidden_two_part.astype(jnp.bfloat16), "tensor").astype(jnp.float32)
    grad_mid = upstream16.astype(jnp.float32) + root_mean_square_backward(
        grad_hidden_two, gain_two, normed_two, inverse_two
    )
    grad_mid16 = grad_mid.astype(jnp.bfloat16)
    grad_output = contract_rows(grad_mid16, out_flat)
    grad_out16 = (
        jnp.dot(grad_mid16, output_matrix, preferred_element_type=jnp.float32)
        .astype(jnp.bfloat16)
        .reshape(count, heads_local, HEAD_SIZE)
    )
    grad_query_rows, grad_keys_all, grad_values_all = attend_backward(
        query_rows,
        keys_all,
        values_all,
        out_rows,
        log_total,
        group_rows(grad_out16, group_count),
        row_pos,
    )
    key_gradient, value_gradient = (
        lax.psum_scatter(
            grad_keys_all.astype(jnp.bfloat16), "seq", scatter_dimension=0, tiled=True
        ).astype(jnp.float32),
        lax.psum_scatter(
            grad_values_all.astype(jnp.bfloat16), "seq", scatter_dimension=0, tiled=True
        ).astype(jnp.float32),
    )
    grad_query = rotate_back(ungroup_rows(grad_query_rows, group_count), cosine, sine_table)
    key_gradient = rotate_back(key_gradient.reshape(count, kv_local, HEAD_SIZE), cosine, sine_table)
    head_part = jnp.stack(
        [
            jnp.sum(grad_query * query_hat, axis=(0, 1)),
            jnp.sum(key_gradient * key_normalized, axis=(0, 1)),
        ],
        axis=0,
    )
    grad_query16 = (
        root_mean_square_backward(grad_query, head_norm_gains[0], query_hat, query_inverse)
        .reshape(count, heads_local * HEAD_SIZE)
        .astype(jnp.bfloat16)
    )
    key_gradient16 = (
        root_mean_square_backward(
            key_gradient, head_norm_gains[1], key_normalized, key_inverse_norm
        )
        .reshape(count, kv_local * HEAD_SIZE)
        .astype(jnp.bfloat16)
    )
    value_gradient16 = value_gradient.astype(jnp.bfloat16)
    grad_querymat = contract_rows(hidden_first, grad_query16)
    grad_keyvalue = jnp.stack(
        [
            contract_rows(hidden_first, key_gradient16),
            contract_rows(hidden_first, value_gradient16),
        ],
        axis=1,
    )
    hidden_one_part = (
        contract_cols(grad_query16, query_matrix)
        + contract_cols(key_gradient16, key_value_matrix[:, 0, :])
        + contract_cols(value_gradient16, key_value_matrix[:, 1, :])
    )
    grad_hidden_one, head_tensor = (
        lax.psum(hidden_one_part.astype(jnp.bfloat16), "tensor").astype(jnp.float32),
        lax.psum(head_part.astype(jnp.bfloat16), "tensor").astype(jnp.float32),
    )
    input_row = grad_mid + root_mean_square_backward(
        grad_hidden_one, gain_one, normed_one, inverse_one
    )
    grad_gains = jnp.stack(
        [
            jnp.sum(grad_hidden_one * normed_one, axis=0),
            jnp.sum(grad_hidden_two * normed_two, axis=0),
        ],
        axis=1,
    )
    return (
        input_row,
        (grad_querymat, grad_keyvalue, grad_output, grad_gateup, grad_down, grad_gains),
        head_tensor,
    )


def body(
    block_input,
    upstream_grad,
    query_weight,
    key_value_weight,
    output_weight,
    gateup_weight,
    down_weight,
    norm_gains,
    head_norm_gains,
    query_momentum,
    query_variance,
    key_value_momentum,
    key_value_variance,
    output_momentum,
    output_variance,
    gateup_momentum,
    gateup_variance,
    down_momentum,
    down_variance,
    norm_momentum,
    norm_variance,
    head_momentum,
    head_variance,
):
    masters = (
        query_weight,
        key_value_weight,
        output_weight,
        gateup_weight,
        down_weight,
        norm_gains,
    )
    shards = tuple((master.astype(jnp.bfloat16) for master in masters))
    gathered = jax.tree.map(
        lambda part, own: part.astype(own.dtype),
        lax.all_gather(as_sent(shards), ("dp", "seq"), axis=0, tiled=True),
        shards,
    )
    query_matrix, key_value_matrix, output_matrix, gateup_matrix, down_matrix, gain_table = gathered
    gain_table = gain_table.astype(jnp.float32)
    weights = (
        query_matrix,
        key_value_matrix,
        output_matrix,
        gateup_matrix,
        down_matrix,
        gain_table[:, 0],
        gain_table[:, 1],
    )
    group_count = QUERY_HEADS // KEY_VALUE_HEADS
    count = block_input.shape[1]
    positions = lax.axis_index("seq") * count + jnp.arange(count, dtype=jnp.int32)
    cosine, sine_table = rope_tables(positions, HEAD_SIZE)
    row_pos = jnp.tile(positions, group_count)
    which = 0
    output16, saved = forward_one(
        block_input[which], weights, head_norm_gains, cosine, sine_table, row_pos
    )
    outputs = [output16]
    saved_all = [saved]
    block_output = jnp.stack(outputs, axis=0)
    which = 0
    input_row, grads, head_piece = backward_one(
        upstream_grad[which],
        saved_all[which],
        weights,
        head_norm_gains,
        cosine,
        sine_table,
        row_pos,
    )
    input_rows = [input_row]
    input_grad = jnp.stack(input_rows, axis=0)
    head_grad = lax.psum(head_piece, ("dp", "seq"))
    owned = jax.tree.map(
        lambda part: part.astype(jnp.float32),
        lax.psum_scatter(as_sent(grads), ("dp", "seq"), scatter_dimension=0, tiled=True),
    )
    grad_q, grad_kv, grad_o, grad_gu, grad_d, grad_n = owned
    new_q = adamw(query_weight, query_momentum, query_variance, grad_q, decay_rate)
    new_kv = adamw(key_value_weight, key_value_momentum, key_value_variance, grad_kv, decay_rate)
    new_o = adamw(output_weight, output_momentum, output_variance, grad_o, decay_rate)
    new_gu = adamw(gateup_weight, gateup_momentum, gateup_variance, grad_gu, decay_rate)
    new_d = adamw(down_weight, down_momentum, down_variance, grad_d, decay_rate)
    new_n = adamw(norm_gains, norm_momentum, norm_variance, grad_n, 0.0)
    new_h = adamw(head_norm_gains, head_momentum, head_variance, head_grad, 0.0)
    return (
        block_output,
        input_grad,
        grad_q,
        grad_kv,
        grad_o,
        grad_gu,
        grad_d,
        grad_n,
        head_grad,
        new_q[0],
        new_kv[0],
        new_o[0],
        new_gu[0],
        new_d[0],
        new_n[0],
        new_h[0],
        new_q[1],
        new_q[2],
        new_kv[1],
        new_kv[2],
        new_o[1],
        new_o[2],
        new_gu[1],
        new_gu[2],
        new_d[1],
        new_d[2],
        new_n[1],
        new_n[2],
        new_h[1],
        new_h[2],
    )


def solution(mesh):
    in_specs = (
        P("dp", "seq", None),
        P("dp", "seq", None),
        P(("dp", "seq"), "tensor"),
        P(("dp", "seq"), None, "tensor"),
        P(("dp", "seq"), "tensor"),
        P(("dp", "seq"), None, "tensor"),
        P(("dp", "seq"), "tensor"),
        P(("dp", "seq"), None),
        P(),
        P(("dp", "seq"), "tensor"),
        P(("dp", "seq"), "tensor"),
        P(("dp", "seq"), None, "tensor"),
        P(("dp", "seq"), None, "tensor"),
        P(("dp", "seq"), "tensor"),
        P(("dp", "seq"), "tensor"),
        P(("dp", "seq"), None, "tensor"),
        P(("dp", "seq"), None, "tensor"),
        P(("dp", "seq"), "tensor"),
        P(("dp", "seq"), "tensor"),
        P(("dp", "seq"), None),
        P(("dp", "seq"), None),
        P(),
        P(),
    )
    out_specs = (
        P("dp", "seq", None),
        P("dp", "seq", None),
        P(("dp", "seq"), "tensor"),
        P(("dp", "seq"), None, "tensor"),
        P(("dp", "seq"), "tensor"),
        P(("dp", "seq"), None, "tensor"),
        P(("dp", "seq"), "tensor"),
        P(("dp", "seq"), None),
        P(),
        P(("dp", "seq"), "tensor"),
        P(("dp", "seq"), None, "tensor"),
        P(("dp", "seq"), "tensor"),
        P(("dp", "seq"), None, "tensor"),
        P(("dp", "seq"), "tensor"),
        P(("dp", "seq"), None),
        P(),
        P(("dp", "seq"), "tensor"),
        P(("dp", "seq"), "tensor"),
        P(("dp", "seq"), None, "tensor"),
        P(("dp", "seq"), None, "tensor"),
        P(("dp", "seq"), "tensor"),
        P(("dp", "seq"), "tensor"),
        P(("dp", "seq"), None, "tensor"),
        P(("dp", "seq"), None, "tensor"),
        P(("dp", "seq"), "tensor"),
        P(("dp", "seq"), "tensor"),
        P(("dp", "seq"), None),
        P(("dp", "seq"), None),
        P(),
        P(),
    )
    return jax.shard_map(body, mesh=mesh, in_specs=in_specs, out_specs=out_specs, check_vma=False)
```

profile of v0, /device:TPU:0, one launch (start us, length us, event | category | flops | bytes accessed | tf_op | source)
XLA Modules:
  0.0 1221.0 jit_solution(6764216487376119563)
XLA Ops:
  8.9 66.7 %all-gather = bf16[32,32,2]{1,2,0:T(2,128)(2,1)S(1)} all-gather(bf16[1,32,2]{1,2,0:T(2,128)(2,1)S(1)} %convert_bitcast_fusion.3), channel_id=1, replica_groups=mesh['dp'=2,'seq'=16,'tensor'=4] {'dp','seq'}, dimensions={0}, use_global_device_ids=true | all-gather | bytes 4224 | tf_op jit(solution)/shard_map/all_gather | solution.py:490
  77.7 64.3 %all_gather.25 = bf16[1024,2,128]{2,0,1:T(8,128)(2,1)S(1)} all-gather(bf16[32,2,128]{2,0,1:T(8,128)(2,1)S(1)} %copy.320), channel_id=1, replica_groups=mesh['dp'=2,'seq'=16,'tensor'=4] {'dp','seq'}, dimensions={0}, use_global_device_ids=true | all-gather | bytes 540672 | tf_op jit(solution)/shard_map/all_gather | solution.py:490
  145.0 67.0 %all_gather.27 = bf16[1024,256]{1,0:T(8,128)(2,1)S(1)} all-gather(bf16[32,256]{1,0:T(8,128)(2,1)S(1)} %convert_element_type.211), channel_id=1, replica_groups=mesh['dp'=2,'seq'=16,'tensor'=4] {'dp','seq'}, dimensions={0}, use_global_device_ids=true | all-gather | bytes 540672 | tf_op jit(solution)/shard_map/all_gather | solution.py:490
  214.1 68.8 %all_gather.29 = bf16[1024,256]{1,0:T(8,128)(2,1)} all-gather(bf16[32,256]{1,0:T(8,128)(2,1)S(1)} %convert_element_type.214), channel_id=1, replica_groups=mesh['dp'=2,'seq'=16,'tensor'=4] {'dp','seq'}, dimensions={0}, use_global_device_ids=true | all-gather | bytes 540672 | tf_op jit(solution)/shard_map/all_gather | solution.py:490
  285.9 3.9 reshape.399
  289.8 3.5 copy.259
  293.3 19.0 %while.33 = (s32[]{:T(128)}, f32[2,512]{1,0:T(2,128)S(1)}, f32[2,512]{1,0:T(2,128)S(1)}, f32[2,512,64]{1,2,0:T(8,128)S(1)}, s32[8]{0:T(128)S(1)}, /*index=5*/s32...) while((s32[]{:T(128)}, f32[2,512]{1,0:T(2,128)S(1)}, ...), condition=%wide.region_9.10_spmd.clone, body=%wide.region_4.9_spmd.clone.sunk | while | flops 138283520 | bytes 7813407 | solution.py:158
  295.2 3.6 conditional.6
  315.4 68.1 %all-reduce.5.cloned.1.call-done = f32[256,1024]{1,0:T(8,128)} async-done(((f32[256,1024]{1,0:T(8,128)}), f32[256,1024]{1,0:T(8,128)}) %all-reduce.5.cloned.1.call-update) | async-done | bytes 1048592 | tf_op jit(solution)/shard_map/psum | solution.py:282
  388.1 3.6 fusion.34
  391.8 3.6 fusion.36
  395.4 39.4 %all-gather.12.cloned.1.call-done = bf16[1024,1152]{1,0:T(8,128)(2,1)} async-done(((bf16[32,1152]{1,0:T(8,128)(2,1)}), bf16[1024,1152]{1,0:T(8,128)(2,1)}) %all-gather.12.cloned.1.call-update) | async-done | bytes 2359312 | tf_op jit(solution)/shard_map/all_gather | solution.py:490
  434.8 4.3 multiply_convert_fusion
  442.0 3.4 fusion.47
  446.2 41.5 %all-reduce.7.cloned.1.call-done = bf16[256,1024]{1,0:T(8,128)(2,1)} async-done(((bf16[256,1024]{1,0:T(8,128)(2,1)}), bf16[256,1024]{1,0:T(8,128)(2,1)}) %all-reduce.7.cloned.1.call-update) | async-done | bytes 524304 | tf_op jit(solution)/shard_map/psum | solution.py:370
  492.3 32.2 %while.34 = (s32[]{:T(128)}, f32[2,512,64]{1,2,0:T(8,128)S(1)}, bf16[8,512,2,64]{1,3,2,0:T(8,128)(2,1)}, bf16[8,512,2,64]{1,3,2,0:T(8,128)(2,1)}, s32[8]{0:T(128...) while((s32[]{:T(128)}, f32[2,512,64]{1,2,0:T(8,128)S(1)}, ...), condition=%wide.region_19.20_spmd.clone, body=%wide.region_16.19_spmd.clone.sunk | while | flops 340263424 | bytes 12213535 | solution.py:220
  494.9 5.5 conditional.7
  531.2 3.6 convolution_convert_fusion.5
  536.3 103.4 %reduce-scatter.13.cloned.1.call-done = bf16[256,128]{0,1:T(8,128)(2,1)} async-done(((bf16[4096,128]{0,1:T(8,128)(2,1)}), bf16[256,128]{0,1:T(8,128)(2,1)}) %reduce-scatter.13.cloned.1.call-update) | async-done | bytes 65552 | tf_op jit(solution)/shard_map/reduce_scatter | solution.py:391
  644.3 71.4 %reduce-scatter.15.cloned.1.call-done = bf16[256,128]{0,1:T(8,128)(2,1)} async-done(((bf16[4096,128]{0,1:T(8,128)(2,1)}), bf16[256,128]{0,1:T(8,128)(2,1)}) %reduce-scatter.15.cloned.1.call-update) | async-done | bytes 65552 | tf_op jit(solution)/shard_map/reduce_scatter | solution.py:394
  722.9 3.3 fusion.32
  726.2 4.3 copy.287
  731.6 3.5 fusion.30
  737.3 26.6 %all-reduce.9.cloned.1.call-done = (bf16[256,1024]{1,0:T(8,128)(2,1)}, bf16[256,1024]{1,0:T(8,128)(2,1)}) async-done(((bf16[256,1024]{1,0:T(8,128)(2,1)}, bf16[256,1024]{1,0:T(8,128)(2,1)}), (bf16[256,1024]{1,0:T(8,128)(2,1)}, bf16[256,1024]{1,0:T(8,128)(2,1)})) %all-reduce.9.cloned.1.call-update) | async-done | bytes 1048592 | tf_op jit(solution)/shard_map/psum | solution.py:291
  766.5 5.0 pad_maximum_fusion
  771.5 27.1 %reduce-scatter.17.cloned.1.call-done = bf16[32,256]{1,0:T(8,128)(2,1)} async-done(((bf16[1024,256]{1,0:T(8,128)(2,1)}), bf16[32,256]{1,0:T(8,128)(2,1)}) %reduce-scatter.17.cloned.1.call-update) | async-done | bytes 16400 | tf_op jit(solution)/shard_map/reduce_scatter | solution.py:531
  800.1 78.5 %reduce-scatter.21.cloned.1.call-done = bf16[32,256]{1,0:T(8,128)(2,1)} async-done(((bf16[1024,256]{1,0:T(8,128)(2,1)}), bf16[32,256]{1,0:T(8,128)(2,1)}) %reduce-scatter.21.cloned.1.call-update) | async-done | bytes 16400 | tf_op jit(solution)/shard_map/reduce_scatter | solution.py:531
  880.7 10.4 psum.46
  891.1 63.9 %psum.47 = f32[2,64]{1,0:T(2,128)S(1)} all-reduce(bf16[2,64]{1,0:T(2,128)(2,1)S(1)} %psum.46), channel_id=1, replica_groups=mesh['dp'=2,'seq'=16,'tensor'=4] {'dp','seq'}, use_global_device_ids=true, to_apply=%region_37.38 | all-reduce | flops 128 | bytes 768 | tf_op jit(solution)/shard_map/psum | solution.py:528
  962.6 78.2 %reduce-scatter.25.cloned.1.call-done = bf16[32,1152]{1,0:T(8,128)(2,1)} async-done(((bf16[1024,1152]{1,0:T(8,128)(2,1)}), bf16[32,1152]{1,0:T(8,128)(2,1)}) %reduce-scatter.25.cloned.1.call-update) | async-done | bytes 73744 | tf_op jit(solution)/shard_map/reduce_scatter | solution.py:531
  1045.2 76.2 %reduce-scatter.27.cloned.1.call-done = bf16[32,2]{1,0:T(8,128)(2,1)} async-done(((bf16[1024,2]{1,0:T(8,128)(2,1)}), bf16[32,2]{1,0:T(8,128)(2,1)}) %reduce-scatter.27.cloned.1.call-update) | async-done | bytes 144
  1122.7 85.7 %reduce-scatter.23.cloned.1.call-done = bf16[32,2,1152]{2,0,1:T(8,128)(2,1)} async-done(((bf16[1024,2,1152]{2,0,1:T(8,128)(2,1)}), bf16[32,2,1152]{2,0,1:T(8,128)(2,1)}) %reduce-scatter.23.cloned.1.call-update) | async-done | bytes 147472 | tf_op jit(solution)/shard_map/reduce_scatter | solution.py:531
  (311 shorter events, 104.1 us)
Async XLA Ops:
  8.0 134.2 %copy-start = (bf16[1,256,1024]{2,1,0:T(8,128)(2,1)S(1)}, bf16[1,256,1024]{2,1,0:T(8,128)(2,1)}, u32[]{:S(2)}) copy-start(bf16[1,256,1024]{2,1,0:T(8,128)(2,1)} %param.31) | copy-start | bytes 1572868
  8.0 134.6 %copy-start.45 = (f32[2,64]{1,0:T(2,128)S(1)}, f32[2,64]{1,0:T(2,128)}, u32[]{:S(2)}) copy-start(f32[2,64]{1,0:T(2,128)} %param.39) | copy-start | bytes 1540
  8.1 274.9 %all-gather.6.cloned.1.call-start = ((), (), s32[]{:S(2)}) async-start(), calls=%async_computation.8 | async-start | bytes 1114112 | tf_op jit(solution)/shard_map/all_gather | solution.py:276
  76.9 135.4 %copy-start.38 = (f32[256]{0:T(256)}, f32[256]{0:T(256)S(1)}, u32[]{:S(2)}) copy-start(f32[256]{0:T(256)S(1)} %add_rsqrt_fusion.3) | copy-start | bytes 3076
  143.9 142.0 %all-gather.8.cloned.1.call-start = ((), (), s32[]{:S(2)}) async-start(), calls=%async_computation.9 | async-start | bytes 1114112 | tf_op jit(solution)/shard_map/all_gather | solution.py:277
  144.9 238.6 %all-reduce.5.cloned.1.call-start = ((), (), s32[]{:S(2)}) async-start(), calls=%async_computation.10 | async-start | bytes 2097152 | tf_op jit(solution)/shard_map/psum | solution.py:282
  313.9 74.3 %all-gather.10.cloned.1.call-start = ((), (), s32[]{:S(2)}) async-start(), calls=%async_computation.11 | async-start | bytes 4866048 | tf_op jit(solution)/shard_map/all_gather | solution.py:490
  314.6 120.1 %all-gather.12.cloned.1.call-start = ((), (), s32[]{:S(2)}) async-start(), calls=%async_computation.12 | async-start | bytes 2433024 | tf_op jit(solution)/shard_map/all_gather | solution.py:490
  315.4 172.3 %all-reduce.7.cloned.1.call-start = ((), (), s32[]{:S(2)}) async-start(), calls=%async_computation.13 | async-start | bytes 1048576 | tf_op jit(solution)/shard_map/psum | solution.py:370
  445.4 194.3 %reduce-scatter.13.cloned.1.call-start = ((), (), s32[]{:S(2)}) async-start(), calls=%async_computation.14 | async-start | bytes 1114112 | tf_op jit(solution)/shard_map/reduce_scatter | solution.py:391
  527.9 187.9 %reduce-scatter.15.cloned.1.call-start = ((), (), s32[]{:S(2)}) async-start(), calls=%async_computation.15 | async-start | bytes 1114112 | tf_op jit(solution)/shard_map/reduce_scatter | solution.py:394
  531.1 232.8 %all-reduce.9.cloned.1.call-start = ((), (), s32[]{:S(2)}) async-start(), calls=%async_computation.22 | async-start | bytes 2097152 | tf_op jit(solution)/shard_map/psum | solution.py:291
  534.8 105.8 %copy-start.37 = (f32[256,2]{0,1:T(2,128)S(1)}, f32[256,2]{0,1:T(2,128)}, u32[]{:S(2)}) copy-start(f32[256,2]{0,1:T(2,128)} %copy-done.36) | copy-start | bytes 6148
  534.8 105.8 %copy-start.41 = (f32[64]{0:T(128)S(1)}, f32[64]{0:T(128)}, u32[]{:S(2)}) copy-start(f32[64]{0:T(128)} %copy-done.40) | copy-start | bytes 772
  536.3 180.8 %copy-start.2 = (bf16[1024,256]{1,0:T(8,128)(2,1)S(1)}, bf16[1024,256]{1,0:T(8,128)(2,1)}, u32[]{:S(2)}) copy-start(bf16[1024,256]{1,0:T(8,128)(2,1)} %copy-done.1) | copy-start | bytes 1572868
  642.0 75.1 %copy-start.28 = (bf16[256,4,64]{0,2,1:T(8,128)(2,1)S(1)}, bf16[256,4,64]{0,2,1:T(8,128)(2,1)}, u32[]{:S(2)}) copy-start(bf16[256,4,64]{0,2,1:T(8,128)(2,1)} %multiply_convert_fusion.4) | copy-start | bytes 393220
  718.3 80.3 %reduce-scatter.17.cloned.1.call-start = ((), (), s32[]{:S(2)}) async-start(), calls=%async_computation.16 | async-start | bytes 540672 | tf_op jit(solution)/shard_map/reduce_scatter | solution.py:531
  719.7 158.9 %reduce-scatter.21.cloned.1.call-start = ((), (), s32[]{:S(2)}) async-start(), calls=%async_computation.18 | async-start | bytes 540672 | tf_op jit(solution)/shard_map/reduce_scatter | solution.py:531
  720.9 237.6 %reduce-scatter.19.cloned.1.call-start = ((), (), s32[]{:S(2)}) async-start(), calls=%async_computation.17 | async-start | bytes 540672 | tf_op jit(solution)/shard_map/reduce_scatter | solution.py:531
  722.8 318.0 %reduce-scatter.25.cloned.1.call-start = ((), (), s32[]{:S(2)}) async-start(), calls=%async_computation.20 | async-start | bytes 2433024 | tf_op jit(solution)/shard_map/reduce_scatter | solution.py:531
  730.5 390.8 %reduce-scatter.27.cloned.1.call-start = ((), (), s32[]{:S(2)}) async-start(), calls=%async_computation.21 | async-start | bytes 270336
  766.4 442.1 %reduce-scatter.23.cloned.1.call-start = ((), (), s32[]{:S(2)}) async-start(), calls=%async_computation.19 | async-start | bytes 4866048 | tf_op jit(solution)/shard_map/reduce_scatter | solution.py:531
  771.5 107.1 %copy-start.33 = (f32[32,256]{1,0:T(8,128)S(1)}, f32[32,256]{1,0:T(8,128)}, u32[]{:S(2)}) copy-start(f32[32,256]{1,0:T(8,128)} %param.35) | copy-start | bytes 98308
  771.5 183.5 %copy-start.46 = (f32[2,64]{1,0:T(2,128)S(1)}, f32[2,64]{1,0:T(2,128)}, u32[]{:S(2)}) copy-start(f32[2,64]{1,0:T(2,128)} %param.39) | copy-start | bytes 1540
  771.5 187.0 %copy-start.34 = (f32[32,2,128]{2,1,0:T(2,128)S(1)}, f32[32,2,128]{2,1,0:T(2,128)}, u32[]{:S(2)}) copy-start(f32[32,2,128]{2,1,0:T(2,128)} %param.34) | copy-start | bytes 98308
  771.5 269.3 %copy-start.23 = (f32[32,1152]{1,0:T(8,128)S(1)}, f32[32,1152]{1,0:T(8,128)}, u32[]{:S(2)}) copy-start(f32[32,1152]{1,0:T(8,128)} %param.37) | copy-start | bytes 442372
  771.5 269.3 %copy-start.29 = (f32[32,1152]{1,0:T(8,128)S(1)}, f32[32,1152]{1,0:T(8,128)}, u32[]{:S(2)}) copy-start(f32[32,1152]{1,0:T(8,128)} %param.48) | copy-start | bytes 442372
  771.5 271.1 %copy-start.13 = (bf16[256,1024]{1,0:T(8,128)(2,1)S(1)}, bf16[256,1024]{1,0:T(8,128)(2,1)}, u32[]{:S(2)}) copy-start(bf16[256,1024]{1,0:T(8,128)(2,1)} %get-tuple-element.762) | copy-start | bytes 1572868
  1042.6 79.6 %copy-start.47 = (f32[32,2]{0,1:T(2,128)S(1)}, f32[32,2]{0,1:T(2,128)}, u32[]{:S(2)}) copy-start(f32[32,2]{0,1:T(2,128)} %param.38) | copy-start | bytes 772
  1042.6 79.6 %copy-start.48 = (f32[32,2]{0,1:T(2,128)S(1)}, f32[32,2]{0,1:T(2,128)}, u32[]{:S(2)}) copy-start(f32[32,2]{0,1:T(2,128)} %param.50) | copy-start | bytes 772
  1042.6 79.5 %copy-start.49 = (f32[32,2]{0,1:T(2,128)S(1)}, f32[32,2]{0,1:T(2,128)}, u32[]{:S(2)}) copy-start(f32[32,2]{0,1:T(2,128)} %param.51) | copy-start | bytes 772
  1042.6 165.9 %copy-start.15 = (f32[32,2,1152]{2,1,0:T(2,128)S(1)}, f32[32,2,1152]{2,1,0:T(2,128)}, u32[]{:S(2)}) copy-start(f32[32,2,1152]{2,1,0:T(2,128)} %param.36) | copy-start | bytes 884740
  (34 other events, 437.3 us)
Sparse Core Ops, SparseCore 0:
  144.0 42.2 all-gather.5
  189.0 42.1 all-gather.7
  314.0 69.4 all-reduce.4
  445.5 42.1 all-reduce.6
  528.0 111.6 reduce-scatter.12
  643.4 72.3 reduce-scatter.14
  718.9 45.0 all-reduce.8
Sparse Core Ops, SparseCore 1:
  317.5 70.6 all-gather.9
  391.1 43.6 all-gather.11
  722.3 76.4 reduce-scatter.16
  802.1 76.4 reduce-scatter.20
  882.0 76.4 reduce-scatter.18
  962.1 78.6 reduce-scatter.24
  1045.0 76.3 reduce-scatter.26
  1125.4 83.0 reduce-scatter.22
where the time goes:
time: 1220 us
  waiting for transfers between devices  702 us (58%)
  blocking collectives  341 us (28%)
  local copies, waits for them, and re-layouts  54.6 us (4%)
  matrix products  50.3 us (4%)
  other arithmetic  34.1 us (3%)
  loops' own time  21.6 us (2%)
  between operations  16.5 us (1%)
    reduce_scatter x5, waiting for transfers between devices, body(): lax.psum_scatter(as_sent(grads), ('dp', 'seq'), scatter_dimension=0, tile...  272 us
    all_gather x4, blocking collectives, body(): lax.all_gather(as_sent(shards), ('dp', 'seq'), axis=0, tiled=True)  267 us
    reduce_scatter x1, waiting for transfers between devices, backward_one(): lax.psum_scatter(grad_keys_all.astype(jnp.bfloat16), 'seq', scatter_dimen...  103 us
    unnamed x16, waiting for transfers between devices  76.4 us
    reduce_scatter x1, waiting for transfers between devices, backward_one(): lax.psum_scatter(grad_values_all.astype(jnp.bfloat16), 'seq', scatter_dim...  71.4 us
    psum x1, waiting for transfers between devices, forward_one(): attn_sum = lax.psum(contract_cols(out_flat, output_matrix), 'tensor')  68.1 us
    psum x1, blocking collectives, body(): head_grad = lax.psum(head_piece, ('dp', 'seq'))  63.9 us
    all_gather x2, waiting for transfers between devices, body(): lax.all_gather(as_sent(shards), ('dp', 'seq'), axis=0, tiled=True)  42.4 us
  transfers between devices with their start and end apart: 15, of which 13 were waited for; matrix products, arithmetic and copies ran while one was open for 6% of the time, Pallas kernels for 0%

commit v1 on v0

v1 whole, which is shorter than its diff:
```python
import functools

import jax
import jax.numpy as jnp
from jax import lax
from jax.experimental import pallas as pl
from jax.experimental.pallas import tpu as pltpu
from jax.sharding import PartitionSpec as P

f32 = jnp.float32
bf16 = jnp.bfloat16
MESH = pl.DeviceIdType.MESH
norm_eps = 1e-05
rope_base = 1000000.0
beta_one = 0.9
beta_two = 0.95
adam_eps = 1e-08
decay_rate = 0.1
adam_count = 3
LOG2E = 1.4426950408889634
ROWS = 256
HD = 64
SCALE = 0.125
CA = 896
CF = 3456
FFC = 1152
SPLIT_A = 512
SPLIT_F = 1792
VMEM = pl.BlockSpec(memory_space=pltpu.VMEM)
ANY = pl.BlockSpec(memory_space=pl.ANY)


def params(collective_id, megabytes=56):
    return pltpu.CompilerParams(
        collective_id=collective_id,
        has_side_effects=True,
        vmem_limit_bytes=megabytes * 1024 * 1024,
    )


def remote(src, dst, send_sem, recv_sem, device):
    return pltpu.make_async_remote_copy(
        src_ref=src,
        dst_ref=dst,
        send_sem=send_sem,
        recv_sem=recv_sem,
        device_id=device,
        device_id_type=MESH,
    )


def transposed(x, dtype):
    return x.astype(f32).T.astype(dtype)


def dot_nt(a, b):
    return lax.dot_general(a, b, (((1,), (1,)), ((), ())), preferred_element_type=f32)


def dot_nn(a, b):
    return jnp.dot(a, b, preferred_element_type=f32)


def place():
    dp = lax.axis_index("dp")
    seq = lax.axis_index("seq")
    return dp, lax.div(seq, 4), lax.rem(seq, 4)


def plane_barrier(dp, y, z):
    barrier = pltpu.get_barrier_semaphore()
    for r in (1, 2, 3):
        for seq in (lax.rem(y + r, 4) * 4 + z, y * 4 + lax.rem(z + r, 4)):
            pl.semaphore_signal(barrier, inc=1, device_id={"seq": seq}, device_id_type=MESH)
    pl.semaphore_signal(barrier, inc=1, device_id={"dp": 1 - dp}, device_id_type=MESH)
    pl.semaphore_wait(barrier, 7)


def tensor_barrier(ti):
    barrier = pltpu.get_barrier_semaphore()
    for r in (1, 2, 3):
        pl.semaphore_signal(
            barrier, inc=1, device_id={"tensor": lax.rem(ti + r, 4)}, device_id_type=MESH
        )
    pl.semaphore_wait(barrier, 3)


def both_barrier(ti, si):
    barrier = pltpu.get_barrier_semaphore()
    for r in (1, 2, 3):
        pl.semaphore_signal(
            barrier, inc=1, device_id={"tensor": lax.rem(ti + r, 4)}, device_id_type=MESH
        )

    def greet(r, carry):
        pl.semaphore_signal(
            barrier, inc=1, device_id={"seq": lax.rem(si + r, 16)}, device_id_type=MESH
        )
        return carry

    lax.fori_loop(1, 16, greet, 0)
    pl.semaphore_wait(barrier, 18)


def own_rows(ti):
    return pl.ds(pl.multiple_of(ti * 64, 64), 64)


def scatter_copies(part, landing, ss, rs, base, ti):
    copies = []
    for r in (1, 2, 3):
        p = lax.rem(ti + r, 4)
        copies.append(
            remote(
                part.at[own_rows(p)],
                landing.at[r - 1],
                ss.at[base + r - 1],
                rs.at[base + r - 1],
                {"tensor": p},
            )
        )
    return copies


def gather_copies(full, ss, rs, base, ti):
    copies = []
    for r in (1, 2, 3):
        p = lax.rem(ti + r, 4)
        copies.append(
            remote(
                full.at[own_rows(ti)],
                full.at[own_rows(ti)],
                ss.at[base + r - 1],
                rs.at[base + r - 1],
                {"tensor": p},
            )
        )
    return copies


def gather_waits(full, ss, rs, base, ti):
    for r in (1, 2, 3):
        p = lax.rem(ti + 4 - r, 4)
        copy = remote(
            full.at[own_rows(p)],
            full.at[own_rows(p)],
            ss.at[base + r - 1],
            rs.at[base + r - 1],
            {"tensor": p},
        )
        copy.wait_recv()
    for r in (1, 2, 3):
        p = lax.rem(ti + r, 4)
        copy = remote(
            full.at[own_rows(ti)],
            full.at[own_rows(ti)],
            ss.at[base + r - 1],
            rs.at[base + r - 1],
            {"tensor": p},
        )
        copy.wait_send()


def start(copies):
    for copy in copies:
        copy.start()


def wait(copies):
    for copy in copies:
        copy.wait()


def gather_weights_kernel(wa, wf, oa, of, loc, ss, rs):
    dp, y, z = place()
    plane_barrier(dp, y, z)
    arrays = ((wa, oa, SPLIT_A, CA, 0), (wf, of, SPLIT_F, CF, 25))
    local = []
    for n, (own, out, cut, width, base) in enumerate(arrays):
        copy = pltpu.make_async_copy(own, out.at[dp, y, z], loc.at[n])
        copy.start()
        local.append(copy)

    def seq_id(yy, zz):
        return {"seq": lax.rem(yy, 4) * 4 + lax.rem(zz, 4)}

    sibling = {"dp": 1 - dp}

    def first(own, out, cut, width, base, r):
        a = remote(
            own.at[:, pl.ds(0, cut)],
            out.at[dp, y, z, :, pl.ds(0, cut)],
            ss.at[base + r - 1],
            rs.at[base + r - 1],
            seq_id(y + r, z),
        )
        b = remote(
            own.at[:, pl.ds(cut, width - cut)],
            out.at[dp, y, z, :, pl.ds(cut, width - cut)],
            ss.at[base + 3 + r - 1],
            rs.at[base + 3 + r - 1],
            seq_id(y, z + r),
        )
        return a, b

    def second(out, cut, width, base, r, yy, zz):
        src_a = out.at[dp, :, zz, :, pl.ds(0, cut)]
        src_b = out.at[dp, yy, :, :, pl.ds(cut, width - cut)]
        a = remote(
            src_a, src_a, ss.at[base + 6 + r - 1], rs.at[base + 6 + r - 1], seq_id(y, z + r)
        )
        b = remote(
            src_b, src_b, ss.at[base + 9 + r - 1], rs.at[base + 9 + r - 1], seq_id(y + r, z)
        )
        return a, b

    started = []
    for own, out, cut, width, base in arrays:
        for r in (1, 3, 2):
            for copy in first(own, out, cut, width, base, r):
                copy.start()
                started.append(copy)

    def to_sibling(ref, base, k):
        copy = remote(ref, ref, ss.at[base + k], rs.at[base + k], sibling)
        copy.start()
        started.append(copy)

    for copy in local:
        copy.wait()
    for own, out, cut, width, base in arrays:
        to_sibling(out.at[dp, y, z], base, 12)
        for r in (1, 3, 2):
            yy, zz = lax.rem(y + 4 - r, 4), lax.rem(z + 4 - r, 4)
            ref_a = out.at[dp, yy, z, :, pl.ds(0, cut)]
            ref_b = out.at[dp, y, zz, :, pl.ds(cut, width - cut)]
            remote(
                ref_a, ref_a, ss.at[base + r - 1], rs.at[base + r - 1], seq_id(y, z)
            ).wait_recv()
            remote(
                ref_b, ref_b, ss.at[base + 3 + r - 1], rs.at[base + 3 + r - 1], seq_id(y, z)
            ).wait_recv()
            to_sibling(ref_a, base, 13 + r - 1)
            to_sibling(ref_b, base, 16 + r - 1)
        for r in (1, 3, 2):
            for copy in second(out, cut, width, base, r, y, z):
                copy.start()
                started.append(copy)
    for own, out, cut, width, base in arrays:
        for r in (1, 3, 2):
            yy, zz = lax.rem(y + 4 - r, 4), lax.rem(z + 4 - r, 4)
            ref_a = out.at[dp, :, zz, :, pl.ds(0, cut)]
            ref_b = out.at[dp, yy, :, :, pl.ds(cut, width - cut)]
            remote(
                ref_a, ref_a, ss.at[base + 6 + r - 1], rs.at[base + 6 + r - 1], seq_id(y, z)
            ).wait_recv()
            to_sibling(ref_a, base, 19 + r - 1)
            remote(
                ref_b, ref_b, ss.at[base + 9 + r - 1], rs.at[base + 9 + r - 1], seq_id(y, z)
            ).wait_recv()
            to_sibling(ref_b, base, 22 + r - 1)
    other = 1 - dp
    for own, out, cut, width, base in arrays:
        refs = [(12, out.at[other, y, z])]
        for r in (1, 3, 2):
            yy, zz = lax.rem(y + 4 - r, 4), lax.rem(z + 4 - r, 4)
            refs.append((13 + r - 1, out.at[other, yy, z, :, pl.ds(0, cut)]))
            refs.append((16 + r - 1, out.at[other, y, zz, :, pl.ds(cut, width - cut)]))
            refs.append((19 + r - 1, out.at[other, :, zz, :, pl.ds(0, cut)]))
            refs.append((22 + r - 1, out.at[other, yy, :, :, pl.ds(cut, width - cut)]))
        for k, ref in refs:
            remote(ref, ref, ss.at[base + k], rs.at[base + k], sibling).wait_recv()
    for copy in started:
        copy.wait_send()


def gather_weights(wa, wf):
    return pl.pallas_call(
        gather_weights_kernel,
        out_shape=(
            jax.ShapeDtypeStruct((2, 4, 4, 32, CA), bf16),
            jax.ShapeDtypeStruct((2, 4, 4, 32, CF), bf16),
        ),
        in_specs=[VMEM, VMEM],
        out_specs=(ANY, ANY),
        scratch_shapes=[
            pltpu.SemaphoreType.DMA((2,)),
            pltpu.SemaphoreType.DMA((50,)),
            pltpu.SemaphoreType.DMA((50,)),
        ],
        compiler_params=params(1),
        name="gather_weights",
    )(wa, wf)


def head_stack(pieces):
    zero = jnp.zeros((HD, 512), pieces.dtype)
    low = jnp.concatenate([pieces[0:64], pieces[64:128]], axis=1)
    high = jnp.concatenate([pieces[128:192], pieces[192:256]], axis=1)
    top = jnp.concatenate([low, zero], axis=1)
    bottom = jnp.concatenate([zero, high], axis=1)
    return jnp.concatenate([top, bottom], axis=0)


def causal_block():
    keys = lax.broadcasted_iota(jnp.int32, (ROWS, 1024), 0)
    rows = lax.broadcasted_iota(jnp.int32, (ROWS, 1024), 1)
    return keys <= jnp.bitwise_and(rows, ROWS - 1)


def attention_forward_kernel(
    x, wa, hg, cs, h1, qkt, qpad, kv, o16, lse, h2, hres, gains, acc, part, landing, ss, rs, ts, tr
):
    si = lax.axis_index("seq")
    ti = lax.axis_index("tensor")
    both_barrier(ti, si)
    gains[...] = wa[:, 768:896].astype(f32).T[0:8]
    x32 = x[...].astype(f32)
    inverse = lax.rsqrt(jnp.mean(x32 * x32, axis=-1, keepdims=True) + norm_eps)
    h1[...] = (x32 * inverse * gains[0:1]).astype(bf16)
    qkv = dot_nn(h1[...], wa[:, 0:512])
    qk = qkv[:, 0:384].T
    qkt[...] = qk
    cosine, sine = cs[0:32], cs[32:64]
    rotated = []
    for h in range(6):
        one = qk[64 * h : 64 * h + 64]
        hat = one * lax.rsqrt(jnp.mean(one * one, axis=0, keepdims=True) + norm_eps)
        scaled = hat * hg[:, (0 if h < 4 else 1) : (1 if h < 4 else 2)]
        a, b = scaled[0:32], scaled[32:64]
        rotated += [a * cosine - b * sine, b * cosine + a * sine]
    q_all = jnp.concatenate(rotated[0:8], axis=0)
    k_all = jnp.concatenate(rotated[8:12], axis=0)
    kv[si, :, 0:128] = k_all.T.astype(bf16)
    kv[si, :, 128:256] = qkv[:, 384:512].astype(bf16)

    def send(r):
        return remote(kv.at[si], kv.at[si], ss.at[r], rs.at[r], {"seq": si + r})

    def send_one(r, carry):
        send(r).start()
        return carry

    lax.fori_loop(1, 16 - si, send_one, 0)
    qpad[...] = head_stack(q_all.astype(bf16))
    ones = jnp.ones((16, ROWS), bf16)

    def visit(block, diagonal):
        k16 = kv[block, :, 0:128]
        scores = dot_nn(k16, qpad[...])
        p = jnp.exp2(scores * (SCALE * LOG2E))
        if diagonal:
            p = jnp.where(causal_block(), p, 0.0)
        p16 = p.astype(bf16)
        vt = transposed(kv[block, :, 128:256], bf16)
        for j in range(2):
            lhs = jnp.concatenate([vt[64 * j : 64 * j + 64], ones], axis=0)
            out = dot_nn(lhs, p16[:, 512 * j : 512 * j + 512])
            if diagonal:
                acc[j] = out
            else:
                acc[j] += out

    visit(si, True)

    def later(r, carry):
        block = si - r
        remote(kv.at[block], kv.at[block], ss.at[r], rs.at[r], {"seq": block}).wait_recv()
        visit(block, False)
        return carry

    lax.fori_loop(1, si + 1, later, 0)
    pieces = []
    for j in range(2):
        total = acc[j, 64:65]
        out = acc[j, 0:64] / total
        lse[j : j + 1] = jnp.log(total) * LOG2E
        pieces += [out[:, 0:256], out[:, 256:512]]
    o16[...] = jnp.concatenate(pieces, axis=0).T.astype(bf16)
    part[...] = dot_nt(o16[...], wa[:, 512:768]).astype(bf16)
    copies = scatter_copies(part, landing, ts, tr, 0, ti)
    start(copies)
    wait(copies)
    rows = own_rows(ti)
    total = x[rows].astype(f32) + part[rows].astype(f32)
    for r in range(3):
        total += landing[r].astype(f32)
    hres[...] = total
    inverse = lax.rsqrt(jnp.mean(total * total, axis=-1, keepdims=True) + norm_eps)
    h2[rows] = (total * inverse * gains[1:2]).astype(bf16)
    start(gather_copies(h2, ts, tr, 3, ti))

    def send_done(r, carry):
        send(r).wait_send()
        return carry

    lax.fori_loop(1, 16 - si, send_done, 0)
    gather_waits(h2, ts, tr, 3, ti)


def attention_forward(x, wa, hg, cs):
    return pl.pallas_call(
        attention_forward_kernel,
        out_shape=(
            jax.ShapeDtypeStruct((256, 1024), bf16),
            jax.ShapeDtypeStruct((384, 256), f32),
            jax.ShapeDtypeStruct((128, 1024), bf16),
            jax.ShapeDtypeStruct((16, 256, 256), bf16),
            jax.ShapeDtypeStruct((256, 256), bf16),
            jax.ShapeDtypeStruct((2, 512), f32),
            jax.ShapeDtypeStruct((256, 1024), bf16),
            jax.ShapeDtypeStruct((64, 1024), f32),
            jax.ShapeDtypeStruct((8, 1024), f32),
        ),
        in_specs=[VMEM] * 4,
        out_specs=(VMEM,) * 9,
        scratch_shapes=[
            pltpu.VMEM((2, 80, 512), f32),
            pltpu.VMEM((256, 1024), bf16),
            pltpu.VMEM((3, 64, 1024), bf16),
            pltpu.SemaphoreType.DMA((16,)),
            pltpu.SemaphoreType.DMA((16,)),
            pltpu.SemaphoreType.DMA((6,)),
            pltpu.SemaphoreType.DMA((6,)),
        ],
        compiler_params=params(2),
        name="attention_forward",
    )(x, wa, hg, cs)


def feed_forward_kernel(
    h2, dy, wf, hres, gains, out, dres16, dres, gf, n2sum,
    z, dg, du, po, pd, lo, ld, dyt, h2t, ts, tr,
):
    ti = lax.axis_index("tensor")
    tensor_barrier(ti)
    width = 384

    def hidden(c, carry):
        at = pl.multiple_of(c * width, 128)
        gate = dot_nn(h2[...], wf[:, pl.ds(at, width)])
        up = dot_nn(h2[...], wf[:, pl.ds(at + FFC, width)])
        dz = dot_nn(dy[...], wf[:, pl.ds(at + 2 * FFC, width)])
        sigma = jax.nn.sigmoid(gate)
        silu = gate * sigma
        z[:, pl.ds(at, width)] = (silu * up).astype(bf16)
        dg[:, pl.ds(at, width)] = (dz * up * sigma * (1.0 + gate * (1.0 - sigma))).astype(bf16)
        du[:, pl.ds(at, width)] = (dz * silu).astype(bf16)
        return carry

    lax.fori_loop(0, 3, hidden, 0)

    def back(n, carry):
        at = pl.ds(pl.multiple_of(n * 256, 256), 256)
        pd[:, at] = (
            dot_nt(dg[...], wf[at, 0:FFC]) + dot_nt(du[...], wf[at, FFC : 2 * FFC])
        ).astype(bf16)
        po[:, at] = dot_nt(z[...], wf[at, 2 * FFC : 3 * FFC]).astype(bf16)
        return carry

    lax.fori_loop(0, 4, back, 0)
    copies_d = scatter_copies(pd, ld, ts, tr, 0, ti)
    copies_o = scatter_copies(po, lo, ts, tr, 3, ti)
    start(copies_d)
    start(copies_o)
    h2t[...] = transposed(h2[...], bf16)
    dyt[...] = transposed(dy[...], bf16)

    def gate_grads(n, carry):
        at = pl.ds(pl.multiple_of(n * 256, 256), 256)
        gf[at, 0:FFC] = dot_nn(h2t[at], dg[...]).astype(bf16)
        gf[at, FFC : 2 * FFC] = dot_nn(h2t[at], du[...]).astype(bf16)
        return carry

    lax.fori_loop(0, 4, gate_grads, 0)
    wait(copies_d)
    wait(copies_o)
    rows = own_rows(ti)
    dh2 = pd[rows].astype(f32)
    ffn = po[rows].astype(f32)
    for r in range(3):
        dh2 += ld[r].astype(f32)
        ffn += lo[r].astype(f32)
    mid = hres[...]
    out[rows] = (mid + ffn).astype(bf16)
    inverse = lax.rsqrt(jnp.mean(mid * mid, axis=-1, keepdims=True) + norm_eps)
    normed = mid * inverse
    scaled = dh2 * gains[1:2]
    inner = jnp.mean(scaled * normed, axis=-1, keepdims=True)
    grad = dy[rows].astype(f32) + inverse * (scaled - normed * inner)
    dres[...] = grad
    dres16[rows] = grad.astype(bf16)
    start(gather_copies(dres16, ts, tr, 6, ti))
    start(gather_copies(out, ts, tr, 9, ti))
    n2sum[...] = jnp.broadcast_to(jnp.sum(dh2 * normed, axis=0, keepdims=True), (8, 1024))

    def down_grads(n, carry):
        at = pl.ds(pl.multiple_of(n * 256, 256), 256)
        gf[at, 2 * FFC : 3 * FFC] = dot_nn(dyt[at], z[...]).astype(bf16)
        return carry

    lax.fori_loop(0, 4, down_grads, 0)
    gather_waits(dres16, ts, tr, 6, ti)
    gather_waits(out, ts, tr, 9, ti)


def feed_forward(h2, dy, wf, hres, gains):
    return pl.pallas_call(
        feed_forward_kernel,
        out_shape=(
            jax.ShapeDtypeStruct((256, 1024), bf16),
            jax.ShapeDtypeStruct((256, 1024), bf16),
            jax.ShapeDtypeStruct((64, 1024), f32),
            jax.ShapeDtypeStruct((1024, CF), bf16),
            jax.ShapeDtypeStruct((8, 1024), f32),
        ),
        in_specs=[VMEM] * 5,
        out_specs=(VMEM,) * 5,
        scratch_shapes=[
            pltpu.VMEM((256, FFC), bf16),
            pltpu.VMEM((256, FFC), bf16),
            pltpu.VMEM((256, FFC), bf16),
            pltpu.VMEM((256, 1024), bf16),
            pltpu.VMEM((256, 1024), bf16),
            pltpu.VMEM((3, 64, 1024), bf16),
            pltpu.VMEM((3, 64, 1024), bf16),
            pltpu.VMEM((1024, 256), bf16),
            pltpu.VMEM((1024, 256), bf16),
            pltpu.SemaphoreType.DMA((12,)),
            pltpu.SemaphoreType.DMA((12,)),
        ],
        compiler_params=params(3),
        name="feed_forward",
    )(h2, dy, wf, hres, gains)


def attention_backward_kernel(
    x, wa, hg, cs, h1, qkt, qpad, kv, o16, lse, gains, dres16, dres, n2sum,
    ga, input_grad, heads,
    dot_pad, do_nat, q_nat, delta, dq, dkv, dkv_in, part, landing, ig16, small, ss, rs, ts, tr,
):
    si = lax.axis_index("seq")
    ti = lax.axis_index("tensor")
    both_barrier(ti, si)
    do_t = transposed(dot_nn(dres16[...], wa[:, 512:768]).astype(bf16), f32)
    o_t = transposed(o16[...], f32)
    products = do_t * o_t
    sums = [jnp.sum(products[64 * h : 64 * h + 64], axis=0, keepdims=True) for h in range(4)]
    delta[...] = jnp.concatenate(sums, axis=1)
    dot_pad[...] = head_stack(do_t.astype(bf16))
    do_nat[...] = transposed(dot_pad[...], bf16)
    q_nat[...] = transposed(qpad[...], bf16)

    def visit(block, diagonal):
        k16 = kv[block, :, 0:128]
        kt = transposed(k16, bf16)
        scores = dot_nn(k16, qpad[...])
        shift = jnp.concatenate([lse[0:1], lse[1:2]], axis=1)
        p = jnp.exp2(scores * (SCALE * LOG2E) - shift)
        if diagonal:
            p = jnp.where(causal_block(), p, 0.0)
        dp = dot_nn(kv[block, :, 128:256], dot_pad[...])
        ds16 = (p * (dp - delta[...])).astype(bf16)
        dkv[block, :, 0:128] = (dot_nn(ds16, q_nat[...]) * SCALE).astype(bf16)
        dkv[block, :, 128:256] = dot_nn(p.astype(bf16), do_nat[...]).astype(bf16)
        for j in range(2):
            out = dot_nn(kt[64 * j : 64 * j + 64], ds16[:, 512 * j : 512 * j + 512])
            if diagonal:
                dq[j] = out
            else:
                dq[j] += out

    visit(si, True)

    def send(r):
        return remote(dkv.at[si - r], dkv_in.at[r], ss.at[r], rs.at[r], {"seq": si - r})

    def later(r, carry):
        visit(si - r, False)
        send(r).start()
        return carry

    lax.fori_loop(1, si + 1, later, 0)

    hats, inverses = [], []
    for h in range(6):
        one = qkt[64 * h : 64 * h + 64]
        inverse = lax.rsqrt(jnp.mean(one * one, axis=0, keepdims=True) + norm_eps)
        inverses.append(inverse)
        hats.append(one * inverse)
    cosine, sine = cs[0:32], cs[32:64]

    def head_back(gradient, h):
        a, b = gradient[0:32], gradient[32:64]
        normed = jnp.concatenate([a * cosine + b * sine, b * cosine - a * sine], axis=0)
        gain = hg[:, 0:1] if h < 4 else hg[:, 1:2]
        scaled = normed * gain
        inner = jnp.mean(scaled * hats[h], axis=0, keepdims=True)
        return inverses[h] * (scaled - hats[h] * inner), normed * hats[h]

    results, q_products = [], 0.0
    for h in range(4):
        piece = dq[h // 2, :, 256 * (h % 2) : 256 * (h % 2) + 256] * SCALE
        result, product = head_back(piece, h)
        results.append(result)
        q_products = q_products + product
    ga[:, 512:768] = dot_nn(transposed(dres16[...], bf16), o16[...]).astype(bf16)

    def receive(r, total):
        remote(dkv.at[si], dkv_in.at[r], ss.at[r], rs.at[r], {"seq": si}).wait_recv()
        return total + dkv_in[r].astype(f32)

    total = lax.fori_loop(1, 16 - si, receive, dkv[si].astype(f32))
    dkt = total[:, 0:128].T
    k_products = 0.0
    for h in range(2):
        result, product = head_back(dkt[64 * h : 64 * h + 64], 4 + h)
        results.append(result)
        k_products = k_products + product
    dqk = jnp.concatenate(results, axis=0).T.astype(bf16)
    dqkv = jnp.concatenate([dqk, total[:, 128:256].astype(bf16)], axis=1)
    part[...] = dot_nt(dqkv, wa[:, 0:512]).astype(bf16)
    copies = scatter_copies(part, landing, ts, tr, 0, ti)
    start(copies)
    ga[:, 0:512] = dot_nn(transposed(h1[...], bf16), dqkv).astype(bf16)
    head_rows = jnp.concatenate(
        [
            jnp.sum(q_products.T, axis=0, keepdims=True),
            jnp.sum(k_products.T, axis=0, keepdims=True),
            jnp.zeros((1, 896), f32),
        ],
        axis=1,
    )
    wait(copies)
    rows = own_rows(ti)
    dh1 = part[rows].astype(f32)
    for r in range(3):
        dh1 += landing[r].astype(f32)
    x32 = x[rows].astype(f32)
    inverse = lax.rsqrt(jnp.mean(x32 * x32, axis=-1, keepdims=True) + norm_eps)
    normed = x32 * inverse
    scaled = dh1 * gains[0:1]
    inner = jnp.mean(scaled * normed, axis=-1, keepdims=True)
    ig16[rows] = (dres[...] + inverse * (scaled - normed * inner)).astype(bf16)
    start(gather_copies(ig16, ts, tr, 3, ti))
    small[0] = jnp.concatenate(
        [
            jnp.sum(dh1 * normed, axis=0, keepdims=True),
            n2sum[0:1],
            head_rows,
            jnp.zeros((5, 1024), f32),
        ],
        axis=0,
    )

    def small_copy(r):
        return remote(
            small.at[0], small.at[r], ts.at[6 + r - 1], tr.at[6 + r - 1], {"tensor": lax.rem(ti + r, 4)}
        )

    copies = [small_copy(r) for r in (1, 2, 3)]
    start(copies)
    wait(copies)
    sums = small[0] + small[1] + small[2] + small[3]
    ga[:, 768:896] = jnp.concatenate([sums, jnp.zeros((120, 1024), f32)], axis=0).T.astype(bf16)
    heads[...] = jnp.broadcast_to(sums[2:3, 0:128], (8, 128))

    def send_done(r, carry):
        send(r).wait_send()
        return carry

    lax.fori_loop(1, si + 1, send_done, 0)
    gather_waits(ig16, ts, tr, 3, ti)
    input_grad[...] = ig16[...].astype(f32)


def attention_backward(*operands):
    return pl.pallas_call(
        attention_backward_kernel,
        out_shape=(
            jax.ShapeDtypeStruct((1024, CA), bf16),
            jax.ShapeDtypeStruct((256, 1024), f32),
            jax.ShapeDtypeStruct((8, 128), f32),
        ),
        in_specs=[VMEM] * 14,
        out_specs=(VMEM,) * 3,
        scratch_shapes=[
            pltpu.VMEM((128, 1024), bf16),
            pltpu.VMEM((1024, 128), bf16),
            pltpu.VMEM((1024, 128), bf16),
            pltpu.VMEM((1, 1024), f32),
            pltpu.VMEM((2, 64, 512), f32),
            pltpu.VMEM((16, 256, 256), bf16),
            pltpu.VMEM((16, 256, 256), bf16),
            pltpu.VMEM((256, 1024), bf16),
            pltpu.VMEM((3, 64, 1024), bf16),
            pltpu.VMEM((256, 1024), bf16),
            pltpu.VMEM((4, 8, 1024), f32),
            pltpu.SemaphoreType.DMA((16,)),
            pltpu.SemaphoreType.DMA((16,)),
            pltpu.SemaphoreType.DMA((9,)),
            pltpu.SemaphoreType.DMA((9,)),
        ],
        compiler_params=params(4),
        name="attention_backward",
    )(*operands)


def scatter_gradients_kernel(
    ga, gf, heads, fa, ff, hsum,
    sa, sf, ra, rf, wa1, wb1, wf1, xf1, ta, tb, tf, uf, va, vb, vf, yf, hs, hr, ss, rs, hss, hrs,
):
    dp, y, z = place()
    plane_barrier(dp, y, z)
    sibling = {"dp": 1 - dp}

    def seq_id(yy, zz):
        return {"seq": lax.rem(yy, 4) * 4 + lax.rem(zz, 4)}

    arrays = (
        (gf, rf, sf, SPLIT_F, CF, 13, (wf1, tf, vf), (xf1, uf, yf), ff),
        (ga, ra, sa, SPLIT_A, CA, 0, (wa1, ta, va), (wb1, tb, vb), fa),
    )
    started = []
    head_copy = remote(heads, hr.at[0], hss.at[0], hrs.at[0], sibling)
    head_copy.start()
    pair = []
    for g, landing, total, cut, width, base, _, _, _ in arrays:
        copy = remote(g.at[1 - dp], landing, ss.at[base + 12], rs.at[base + 12], sibling)
        copy.start()
        pair.append(copy)
    head_copy.wait()
    hs[0] = heads[...] + hr[0]
    head_z = [
        remote(hs.at[0], hr.at[r], hss.at[r], hrs.at[r], seq_id(y, z + r)) for r in (1, 2, 3)
    ]
    start(head_z)
    for n, (g, landing, total, cut, width, base, half_a, half_b, _) in enumerate(arrays):
        pair[n].wait()

        def add(i, carry):
            yy, zz = lax.div(i, 4), lax.rem(i, 4)
            total[yy, zz] = (
                g[dp, yy, zz].astype(f32) + landing[yy, zz].astype(f32)
            ).astype(bf16)
            return carry

        lax.fori_loop(0, 16, add, 0)
        for r in (2, 1, 3):
            zz, yy = lax.rem(z + r, 4), lax.rem(y + r, 4)
            a = remote(
                total.at[:, zz, :, pl.ds(0, cut)],
                half_a[0].at[r - 1],
                ss.at[base + r - 1],
                rs.at[base + r - 1],
                seq_id(y, z + r),
            )
            b = remote(
                total.at[yy, :, :, pl.ds(cut, width - cut)],
                half_b[0].at[r - 1],
                ss.at[base + 3 + r - 1],
                rs.at[base + 3 + r - 1],
                seq_id(y + r, z),
            )
            a.start()
            b.start()
            started.append((n, 0, a))
            started.append((n, 1, b))
    for copy in head_z:
        copy.wait()
    hs[1] = hs[0] + hr[1] + hr[2] + hr[3]
    head_y = [
        remote(hs.at[1], hr.at[3 + r], hss.at[3 + r], hrs.at[3 + r], seq_id(y + r, z))
        for r in (1, 2, 3)
    ]
    start(head_y)
    final = []
    for n, (g, landing, total, cut, width, base, half_a, half_b, _) in enumerate(arrays):
        for m, half in ((0, half_a), (1, half_b)):
            for k, which, copy in started:
                if (k, which) == (n, m):
                    copy.wait()

            def add(i, carry):
                if m == 0:
                    mine = total[i, z, :, 0:cut]
                else:
                    mine = total[y, i, :, cut:width]
                summed = mine.astype(f32)
                for r in range(3):
                    summed += half[0][r, i].astype(f32)
                half[1][i] = summed.astype(bf16)
                return carry

            lax.fori_loop(0, 4, add, 0)
            for r in (2, 1, 3):
                if m == 0:
                    to, target = lax.rem(y + r, 4), seq_id(y + r, z)
                else:
                    to, target = lax.rem(z + r, 4), seq_id(y, z + r)
                k = base + 6 + 3 * m + r - 1
                copy = remote(half[1].at[to], half[2].at[r - 1], ss.at[k], rs.at[k], target)
                copy.start()
                final.append((n, m, copy))
    for copy in head_y:
        copy.wait()
    hsum[...] = hs[1] + hr[4] + hr[5] + hr[6]
    for n, (g, landing, total, cut, width, base, half_a, half_b, result) in enumerate(arrays):
        for m, half in ((0, half_a), (1, half_b)):
            for k, which, copy in final:
                if (k, which) == (n, m):
                    copy.wait()
            mine = y if m == 0 else z
            summed = half[1][mine].astype(f32)
            for r in range(3):
                summed += half[2][r].astype(f32)
            if m == 0:
                result[:, 0:cut] = summed
            else:
                result[:, cut:width] = summed


def scatter_gradients(ga, gf, heads):
    def block(*shape):
        return pltpu.VMEM(shape, bf16)

    rest_a, rest_f = CA - SPLIT_A, CF - SPLIT_F
    return pl.pallas_call(
        scatter_gradients_kernel,
        out_shape=(
            jax.ShapeDtypeStruct((32, CA), f32),
            jax.ShapeDtypeStruct((32, CF), f32),
            jax.ShapeDtypeStruct((8, 128), f32),
        ),
        in_specs=[VMEM] * 3,
        out_specs=(VMEM,) * 3,
        scratch_shapes=[
            block(4, 4, 32, CA),
            block(4, 4, 32, CF),
            block(4, 4, 32, CA),
            block(4, 4, 32, CF),
            block(3, 4, 32, SPLIT_A),
            block(3, 4, 32, rest_a),
            block(3, 4, 32, SPLIT_F),
            block(3, 4, 32, rest_f),
            block(4, 32, SPLIT_A),
            block(4, 32, rest_a),
            block(4, 32, SPLIT_F),
            block(4, 32, rest_f),
            block(3, 32, SPLIT_A),
            block(3, 32, rest_a),
            block(3, 32, SPLIT_F),
            block(3, 32, rest_f),
            pltpu.VMEM((2, 8, 128), f32),
            pltpu.VMEM((7, 8, 128), f32),
            pltpu.SemaphoreType.DMA((26,)),
            pltpu.SemaphoreType.DMA((26,)),
            pltpu.SemaphoreType.DMA((7,)),
            pltpu.SemaphoreType.DMA((7,)),
        ],
        compiler_params=params(5),
        name="scatter_gradients",
    )(ga.reshape(2, 4, 4, 32, CA), gf.reshape(2, 4, 4, 32, CF), heads)


def adamw(weight, momentum, variance, gradient, decay):
    first = beta_one * momentum + (1.0 - beta_one) * gradient
    second = beta_two * variance + (1.0 - beta_two) * gradient * gradient
    first_fixed = first / (1.0 - beta_one**adam_count)
    second_fixed = second / (1.0 - beta_two**adam_count)
    direction = first_fixed / (jnp.sqrt(second_fixed) + adam_eps) + decay * weight
    return (direction, first, second)


def body(
    block_input,
    upstream_grad,
    query_weight,
    key_value_weight,
    output_weight,
    gateup_weight,
    down_weight,
    norm_gains,
    head_norm_gains,
    query_momentum,
    query_variance,
    key_value_momentum,
    key_value_variance,
    output_momentum,
    output_variance,
    gateup_momentum,
    gateup_variance,
    down_momentum,
    down_variance,
    norm_momentum,
    norm_variance,
    head_momentum,
    head_variance,
):
    x = block_input[0]
    dy = upstream_grad[0]
    wa_own = jnp.concatenate(
        [
            query_weight,
            key_value_weight[:, 0],
            key_value_weight[:, 1],
            output_weight,
            jnp.pad(norm_gains, ((0, 0), (0, 126))),
        ],
        axis=1,
    ).astype(bf16)
    wf_own = jnp.concatenate(
        [gateup_weight[:, 0], gateup_weight[:, 1], down_weight], axis=1
    ).astype(bf16)
    wa, wf = gather_weights(wa_own, wf_own)
    wa = wa.reshape(1024, CA)
    wf = wf.reshape(1024, CF)
    positions = lax.axis_index("seq") * ROWS + jnp.arange(ROWS, dtype=jnp.int32)
    frequency = rope_base ** (-(jnp.arange(HD // 2, dtype=f32) * 2.0) / HD)
    angles = positions.astype(f32)[None, :] * frequency[:, None]
    cs = jnp.concatenate([jnp.cos(angles), jnp.sin(angles)], axis=0)
    hg = head_norm_gains.T
    h1, qkt, qpad, kv, o16, lse, h2, hres, gains = attention_forward(x, wa, hg, cs)
    out, dres16, dres, gf, n2sum = feed_forward(h2, dy, wf, hres, gains)
    ga, input_grad, heads = attention_backward(
        x, wa, hg, cs, h1, qkt, qpad, kv, o16, lse, gains, dres16, dres, n2sum
    )
    fa, ff, hsum = scatter_gradients(ga, gf, heads)
    grad_q = fa[:, 0:256]
    grad_kv = jnp.stack([fa[:, 256:384], fa[:, 384:512]], axis=1)
    grad_o = fa[:, 512:768]
    grad_n = fa[:, 768:770]
    grad_gu = jnp.stack([ff[:, 0:FFC], ff[:, FFC : 2 * FFC]], axis=1)
    grad_d = ff[:, 2 * FFC :]
    head_grad = jnp.stack([hsum[0, 0:64], hsum[0, 64:128]], axis=0)
    new_q = adamw(query_weight, query_momentum, query_variance, grad_q, decay_rate)
    new_kv = adamw(key_value_weight, key_value_momentum, key_value_variance, grad_kv, decay_rate)
    new_o = adamw(output_weight, output_momentum, output_variance, grad_o, decay_rate)
    new_gu = adamw(gateup_weight, gateup_momentum, gateup_variance, grad_gu, decay_rate)
    new_d = adamw(down_weight, down_momentum, down_variance, grad_d, decay_rate)
    new_n = adamw(norm_gains, norm_momentum, norm_variance, grad_n, 0.0)
    new_h = adamw(head_norm_gains, head_momentum, head_variance, head_grad, 0.0)
    return (
        out[None],
        input_grad[None],
        grad_q,
        grad_kv,
        grad_o,
        grad_gu,
        grad_d,
        grad_n,
        head_grad,
        new_q[0],
        new_kv[0],
        new_o[0],
        new_gu[0],
        new_d[0],
        new_n[0],
        new_h[0],
        new_q[1],
        new_q[2],
        new_kv[1],
        new_kv[2],
        new_o[1],
        new_o[2],
        new_gu[1],
        new_gu[2],
        new_d[1],
        new_d[2],
        new_n[1],
        new_n[2],
        new_h[1],
        new_h[2],
    )


def solution(mesh):
    in_specs = (
        P("dp", "seq", None),
        P("dp", "seq", None),
        P(("dp", "seq"), "tensor"),
        P(("dp", "seq"), None, "tensor"),
        P(("dp", "seq"), "tensor"),
        P(("dp", "seq"), None, "tensor"),
        P(("dp", "seq"), "tensor"),
        P(("dp", "seq"), None),
        P(),
        P(("dp", "seq"), "tensor"),
        P(("dp", "seq"), "tensor"),
        P(("dp", "seq"), None, "tensor"),
        P(("dp", "seq"), None, "tensor"),
        P(("dp", "seq"), "tensor"),
        P(("dp", "seq"), "tensor"),
        P(("dp", "seq"), None, "tensor"),
        P(("dp", "seq"), None, "tensor"),
        P(("dp", "seq"), "tensor"),
        P(("dp", "seq"), "tensor"),
        P(("dp", "seq"), None),
        P(("dp", "seq"), None),
        P(),
        P(),
    )
    out_specs = (
        P("dp", "seq", None),
        P("dp", "seq", None),
        P(("dp", "seq"), "tensor"),
        P(("dp", "seq"), None, "tensor"),
        P(("dp", "seq"), "tensor"),
        P(("dp", "seq"), None, "tensor"),
        P(("dp", "seq"), "tensor"),
        P(("dp", "seq"), None),
        P(),
        P(("dp", "seq"), "tensor"),
        P(("dp", "seq"), None, "tensor"),
        P(("dp", "seq"), "tensor"),
        P(("dp", "seq"), None, "tensor"),
        P(("dp", "seq"), "tensor"),
        P(("dp", "seq"), None),
        P(),
        P(("dp", "seq"), "tensor"),
        P(("dp", "seq"), "tensor"),
        P(("dp", "seq"), None, "tensor"),
        P(("dp", "seq"), None, "tensor"),
        P(("dp", "seq"), "tensor"),
        P(("dp", "seq"), "tensor"),
        P(("dp", "seq"), None, "tensor"),
        P(("dp", "seq"), None, "tensor"),
        P(("dp", "seq"), "tensor"),
        P(("dp", "seq"), "tensor"),
        P(("dp", "seq"), None),
        P(("dp", "seq"), None),
        P(),
        P(),
    )
    return jax.shard_map(body, mesh=mesh, in_specs=in_specs, out_specs=out_specs, check_vma=False)
```

time: 1220 us -> 279 us (0.23)
  waiting for transfers between devices: 702 us -> 0 us
  blocking collectives: 341 us -> 0 us
  Pallas kernels: 0 us -> 254 us
  matrix products: 50.3 us -> 0 us
  local copies, waits for them, and re-layouts: 54.6 us -> 14.5 us
  other arithmetic: 34.1 us -> 8.24 us
  loops' own time: 21.6 us -> 0 us
  between operations: 16.5 us -> 1.01 us
    reduce_scatter x7 -> x0, waiting for transfers between devices: 447 us -> none  [the longest x5 272 us: body(): lax.psum_scatter(as_sent(grads), ('dp', 'seq'), scatter_dimension=0, tile...]
    all_gather x4 -> x0, blocking collectives: 267 us -> none  [body(): lax.all_gather(as_sent(shards), ('dp', 'seq'), axis=0, tiled=True)]
    pallas_call x0 -> x5, Pallas kernels: none -> 254 us  [the longest x1 85.6 us: attention_backward(): pl.pallas_call(attention_backward_kernel, out_shape=(jax.ShapeDtypeStruct...]
    psum x3 -> x0, waiting for transfers between devices: 136 us -> none  [the longest x1 68.1 us: forward_one(): attn_sum = lax.psum(contract_cols(out_flat, output_matrix), 'tensor')]
    unnamed x16 -> x0, waiting for transfers between devices: 76.4 us -> none
    psum x2 -> x0, blocking collectives: 74.3 us -> none  [the longest x1 63.9 us: body(): head_grad = lax.psum(head_piece, ('dp', 'seq'))]
    dot_general x28 -> x0, matrix products: 50.3 us -> none  [the longest x7 16.1 us: contract_cols(): lax.dot_general(left, right, (((1,), (1,)), ((), ())), preferred_element_...]
    all_gather x4 -> x0, waiting for transfers between devices: 42.4 us -> none  [the longest x2 42.4 us: body(): lax.all_gather(as_sent(shards), ('dp', 'seq'), axis=0, tiled=True)]
  transfers between devices with their start and end apart: 15 -> 0, of which waited for: 13 -> 0; matrix products, arithmetic and copies ran while one was open for 6% -> 0% of each run, Pallas kernels for 0% -> 0%
where the time goes in v1:
time: 279 us; the launch traced here: 278 us
  Pallas kernels  254 us (91%)
  local copies, waits for them, and re-layouts  14.5 us (5%)
  other arithmetic  8.24 us (3%)
    pallas_call x1, Pallas kernels, attention_backward(): pl.pallas_call(attention_backward_kernel, out_shape=(jax.ShapeDtypeStruct...  85.6 us
    pallas_call x1, Pallas kernels, scatter_gradients(): pl.pallas_call(scatter_gradients_kernel, out_shape=(jax.ShapeDtypeStruct(...  47.5 us
    pallas_call x1, Pallas kernels, gather_weights(): pl.pallas_call(gather_weights_kernel, out_shape=(jax.ShapeDtypeStruct((2,...  45.5 us
    pallas_call x1, Pallas kernels, feed_forward(): pl.pallas_call(feed_forward_kernel, out_shape=(jax.ShapeDtypeStruct((256,...  42.9 us
    pallas_call x1, Pallas kernels, attention_forward(): pl.pallas_call(attention_forward_kernel, out_shape=(jax.ShapeDtypeStruct(...  32.9 us
    unnamed x67, local copies, waits for them, and re-layouts  13.3 us

profile of v1, /device:TPU:0, one launch (start us, length us, event | category | flops | bytes accessed | tf_op | source)
XLA Modules:
  0.0 278.2 jit_solution(14165052196353512472)
XLA Ops:
  0.7 0.8 copy.124
  1.4 0.8 convert_dynamic-update-slice_fusion.1
  2.2 0.8 convert_dynamic-update-slice_fusion
  3.0 0.8 broadcast_multiply_fusion
  3.9 1.0 copy.123
  4.9 0.9 convert.35
  5.8 0.7 pad_maximum_fusion.1.wf
  6.5 45.5 %gather_weights.1 = (bf16[2,4,4,32,896]{4,3,2,1,0:T(8,128)(2,1)}, bf16[2,4,4,32,3456]{4,3,2,1,0:T(8,128)(2,1)}) custom-call(bf16[32,896]{1,0:T(8,128)(2,1)} %copy-done.12, bf16[32,3456]{1,0:T(8,128)(2,1)} %pad_maximum_fusion.1.wf), custom_call_target="tpu_custom_call" | custom-call | tf_op jit(solution)/shard_map/gather_weights/pallas_call | solution.py:278
  52.3 0.6 pad_maximum_fusion.2.cs
  52.9 0.7 copy.84
  53.7 32.9 %attention_forward.1 = (bf16[256,1024]{1,0:T(8,128)(2,1)}, f32[384,256]{1,0:T(8,128)}, bf16[128,1024]{1,0:T(8,128)(2,1)}, bf16[16,256,256]{2,1,0:T(8,128)(2,1)},...) custom-call(bf16[256,1024]{1,0:T(8,128)(2,1)} %bitcast.33, ...), custom_call_target="tpu_custom_call" | custom-call | tf_op jit(solution)/shard_map/attention_forward/pallas_call | solution.py:402
  86.6 42.9 %feed_forward.1 = (bf16[256,1024]{1,0:T(8,128)(2,1)}, bf16[256,1024]{1,0:T(8,128)(2,1)}, f32[64,1024]{1,0:T(8,128)}, bf16[1024,3456]{1,0:T(8,128)(2,1)}, f32[8,1024]{1,0:T(8,128)}) custom-call(bf16[256,1024]{1,0:T(8,128)(2,1)} %get-tuple-element.53.h2, bf16[256,1024]{1,0:T(8,128)(2,1)} %bitcast.37, bf16[1024,3456]{1,0:T(8,128)(2,1)} %bitcast.31, ...), custom_call_target="tpu_custom_call" | custom-call | tf_op jit(solution)/shard_map/feed_forward/pallas_call | solution.py:508
  129.5 85.6 %attention_backward.1 = (bf16[1024,896]{1,0:T(8,128)(2,1)}, f32[256,1024]{1,0:T(8,128)}, f32[8,128]{1,0:T(8,128)}) custom-call(bf16[256,1024]{1,0:T(8,128)(2,1)} %bitcast.34, bf16[1024,896]{1,0:T(8,128)(2,1)} %bitcast.30, f32[64,2]{1,0:T(8,128)} %bitcast.40, f32[64,256]{1,0:T(8,128)} %pad_maximum_fusion.2.cs, bf16[256,1024]{1,0:T(8,128)(2,1)} %get-tuple-element.58.h1, ...), custom_call_target="tpu_custom_call" | custom-call | tf_op jit(solution)/shard_map/attention_backward/pallas_call | solution.py:678
  215.2 47.5 %scatter_gradients.1 = (f32[32,896]{1,0:T(8,128)}, f32[32,3456]{1,0:T(8,128)}, f32[8,128]{1,0:T(8,128)}) custom-call(bf16[2,4,4,32,896]{4,3,2,1,0:T(8,128)(2,1)} %bitcast.35, bf16[2,4,4,32,3456]{4,3,2,1,0:T(8,128)(2,1)} %bitcast.32, f32[8,128]{1,0:T(8,128)} %get-tuple-element.70.heads), custom_call_target="tpu_custom_call" | custom-call | tf_op jit(solution)/shard_map/scatter_gradients/pallas_call | solution.py:828
  262.7 0.8 fusion.18
  263.5 0.6 multiply_add_fusion.9
  264.1 1.9 multiply_add_fusion.1
  266.4 0.9 copy.103
  267.4 0.9 copy.104
  268.3 0.9 copy.96
  269.2 0.9 copy.99
  270.3 0.6 copy.101
  270.9 0.6 copy.102
  271.6 0.6 copy.95
  272.2 0.6 copy.98
  272.9 0.7 multiply_add_fusion.3
  273.9 0.6 copy.100
  274.5 0.6 copy.105
  275.2 0.6 copy.106
  275.8 0.6 copy.97
  276.4 0.8 copy.135
  277.2 1.0 copy.136
  (65 shorter events, 1.1 us)
Async XLA Ops:
  0.7 52.3 %copy-start.19 = (f32[2,64]{1,0:T(2,128)S(1)}, f32[2,64]{1,0:T(2,128)}, u32[]{:S(2)}) copy-start(f32[2,64]{1,0:T(2,128)} %param.31) | copy-start | bytes 1540
  3.9 2.7 copy-start.12
  215.1 48.4 %copy-start.22 = (f32[2,64]{1,0:T(2,128)S(1)}, f32[2,64]{1,0:T(2,128)}, u32[]{:S(2)}) copy-start(f32[2,64]{1,0:T(2,128)} %param.44) | copy-start | bytes 1540
  215.1 48.4 %copy-start.23 = (f32[2,64]{1,0:T(2,128)S(1)}, f32[2,64]{1,0:T(2,128)}, u32[]{:S(2)}) copy-start(f32[2,64]{1,0:T(2,128)} %param.45) | copy-start | bytes 1540
  215.1 49.0 %copy-start.2 = (f32[32,1152]{1,0:T(8,128)S(1)}, f32[32,1152]{1,0:T(8,128)}, u32[]{:S(2)}) copy-start(f32[32,1152]{1,0:T(8,128)} %param.29) | copy-start | bytes 442372
  215.1 49.0 %copy-start.6 = (f32[32,1152]{1,0:T(8,128)S(1)}, f32[32,1152]{1,0:T(8,128)}, u32[]{:S(2)}) copy-start(f32[32,1152]{1,0:T(8,128)} %param.40) | copy-start | bytes 442372
  215.2 49.0 %copy-start.7 = (f32[32,1152]{1,0:T(8,128)S(1)}, f32[32,1152]{1,0:T(8,128)}, u32[]{:S(2)}) copy-start(f32[32,1152]{1,0:T(8,128)} %param.41) | copy-start | bytes 442372
  215.2 50.9 %copy-start = (f32[32,2,1152]{2,1,0:T(2,128)S(1)}, f32[32,2,1152]{2,1,0:T(2,128)}, u32[]{:S(2)}) copy-start(f32[32,2,1152]{2,1,0:T(2,128)} %param.28) | copy-start | bytes 884740
  215.2 50.9 %copy-start.4 = (f32[32,2,1152]{2,1,0:T(2,128)S(1)}, f32[32,2,1152]{2,1,0:T(2,128)}, u32[]{:S(2)}) copy-start(f32[32,2,1152]{2,1,0:T(2,128)} %param.38) | copy-start | bytes 884740
  215.2 50.8 %copy-start.5 = (f32[32,2,1152]{2,1,0:T(2,128)S(1)}, f32[32,2,1152]{2,1,0:T(2,128)}, u32[]{:S(2)}) copy-start(f32[32,2,1152]{2,1,0:T(2,128)} %param.39) | copy-start | bytes 884740
  266.0 4.2 %copy-start.11 = (f32[32,896]{1,0:T(8,128)S(1)}, f32[32,896]{1,0:T(8,128)}, u32[]{:S(2)}) copy-start(f32[32,896]{1,0:T(8,128)} %get-tuple-element.71) | copy-start | bytes 344068
  266.0 4.2 %copy-start.10 = (f32[32,2,128]{2,1,0:T(2,128)S(1)}, f32[32,2,128]{2,1,0:T(2,128)}, u32[]{:S(2)}) copy-start(f32[32,2,128]{2,1,0:T(2,128)} %param.26) | copy-start | bytes 98308
  266.1 4.1 %copy-start.17 = (f32[32,2,128]{2,1,0:T(2,128)S(1)}, f32[32,2,128]{2,1,0:T(2,128)}, u32[]{:S(2)}) copy-start(f32[32,2,128]{2,1,0:T(2,128)} %param.34) | copy-start | bytes 98308
  266.1 4.1 %copy-start.18 = (f32[32,2,128]{2,1,0:T(2,128)S(1)}, f32[32,2,128]{2,1,0:T(2,128)}, u32[]{:S(2)}) copy-start(f32[32,2,128]{2,1,0:T(2,128)} %param.35) | copy-start | bytes 98308
  266.1 6.8 %copy-start.8 = (f32[32,256]{1,0:T(8,128)S(1)}, f32[32,256]{1,0:T(8,128)}, u32[]{:S(2)}) copy-start(f32[32,256]{1,0:T(8,128)} %param.25) | copy-start | bytes 98308
  266.1 6.7 %copy-start.9 = (f32[32,256]{1,0:T(8,128)S(1)}, f32[32,256]{1,0:T(8,128)}, u32[]{:S(2)}) copy-start(f32[32,256]{1,0:T(8,128)} %param.27) | copy-start | bytes 98308
  266.1 6.7 %copy-start.13 = (f32[32,256]{1,0:T(8,128)S(1)}, f32[32,256]{1,0:T(8,128)}, u32[]{:S(2)}) copy-start(f32[32,256]{1,0:T(8,128)} %param.36) | copy-start | bytes 98308
  266.1 6.7 %copy-start.14 = (f32[32,256]{1,0:T(8,128)S(1)}, f32[32,256]{1,0:T(8,128)}, u32[]{:S(2)}) copy-start(f32[32,256]{1,0:T(8,128)} %param.37) | copy-start | bytes 98308
  266.1 6.7 %copy-start.15 = (f32[32,256]{1,0:T(8,128)S(1)}, f32[32,256]{1,0:T(8,128)}, u32[]{:S(2)}) copy-start(f32[32,256]{1,0:T(8,128)} %param.33) | copy-start | bytes 98308
  266.1 6.7 %copy-start.16 = (f32[32,256]{1,0:T(8,128)S(1)}, f32[32,256]{1,0:T(8,128)}, u32[]{:S(2)}) copy-start(f32[32,256]{1,0:T(8,128)} %param.32) | copy-start | bytes 98308
  266.4 7.3 %copy-start.20 = (f32[32,2]{0,1:T(2,128)S(1)}, f32[32,2]{0,1:T(2,128)}, u32[]{:S(2)}) copy-start(f32[32,2]{0,1:T(2,128)} %param.42) | copy-start | bytes 772
  266.4 7.4 %copy-start.21 = (f32[32,2]{0,1:T(2,128)S(1)}, f32[32,2]{0,1:T(2,128)}, u32[]{:S(2)}) copy-start(f32[32,2]{0,1:T(2,128)} %param.43) | copy-start | bytes 772
  266.4 10.0 %copy-start.3 = (bf16[256,1024]{1,0:T(8,128)(2,1)S(1)}, bf16[256,1024]{1,0:T(8,128)(2,1)}, u32[]{:S(2)}) copy-start(bf16[256,1024]{1,0:T(8,128)(2,1)} %get-tuple-element.57) | copy-start | bytes 1572868
  267.4 9.9 %copy-start.1 = (f32[256,1024]{1,0:T(8,128)S(1)}, f32[256,1024]{1,0:T(8,128)}, u32[]{:S(2)}) copy-start(f32[256,1024]{1,0:T(8,128)} %get-tuple-element.67) | copy-start | bytes 3145732

commit v2 on v1

v2 whole, which is shorter than its diff:
```python
import numpy as np
import jax
import jax.numpy as jnp
from jax import lax
from jax.experimental import pallas as pl
from jax.experimental.pallas import tpu as pltpu
from jax.sharding import PartitionSpec as P

f32 = jnp.float32
bf16 = jnp.bfloat16
MESH = pl.DeviceIdType.MESH
norm_eps = 1e-05
rope_base = 1000000.0
beta_one = 0.9
beta_two = 0.95
adam_eps = 1e-08
decay_rate = 0.1
adam_count = 3
LOG2E = 1.4426950408889634
ROWS = 256
HD = 64
SCALE = 0.125
CA = 896
CG = 768
CF = 3456
FFC = 1152
SPLIT_A = 512
SPLIT_G = 384
SPLIT_F = 1792
VMEM = pl.BlockSpec(memory_space=pltpu.VMEM)
ANY = pl.BlockSpec(memory_space=pl.ANY)


def params(collective_id, megabytes=56):
    return pltpu.CompilerParams(
        collective_id=collective_id,
        has_side_effects=True,
        vmem_limit_bytes=megabytes * 1024 * 1024,
    )


def remote(src, dst, send_sem, recv_sem, device):
    return pltpu.make_async_remote_copy(
        src_ref=src,
        dst_ref=dst,
        send_sem=send_sem,
        recv_sem=recv_sem,
        device_id=device,
        device_id_type=MESH,
    )


def transposed(x, dtype):
    return x.astype(f32).T.astype(dtype)


def dot_nt(a, b):
    return lax.dot_general(a, b, (((1,), (1,)), ((), ())), preferred_element_type=f32)


def dot_nn(a, b):
    return jnp.dot(a, b, preferred_element_type=f32)


def place():
    dp = lax.axis_index("dp")
    seq = lax.axis_index("seq")
    return dp, lax.div(seq, 4), lax.rem(seq, 4)


def own_rows(ti):
    return pl.ds(pl.multiple_of(ti * 64, 64), 64)


def scatter_copies(part, landing, ss, rs, base, ti):
    copies = []
    for r in (1, 2, 3):
        p = lax.rem(ti + r, 4)
        copies.append(
            remote(
                part.at[own_rows(p)],
                landing.at[r - 1],
                ss.at[base + r - 1],
                rs.at[base + r - 1],
                {"tensor": p},
            )
        )
    return copies


def gather_copies(full, ss, rs, base, ti):
    copies = []
    for r in (1, 2, 3):
        p = lax.rem(ti + r, 4)
        copies.append(
            remote(
                full.at[own_rows(ti)],
                full.at[own_rows(ti)],
                ss.at[base + r - 1],
                rs.at[base + r - 1],
                {"tensor": p},
            )
        )
    return copies


def gather_waits(full, ss, rs, base, ti):
    for r in (1, 2, 3):
        p = lax.rem(ti + 4 - r, 4)
        copy = remote(
            full.at[own_rows(p)],
            full.at[own_rows(p)],
            ss.at[base + r - 1],
            rs.at[base + r - 1],
            {"tensor": p},
        )
        copy.wait_recv()
    for r in (1, 2, 3):
        p = lax.rem(ti + r, 4)
        copy = remote(
            full.at[own_rows(ti)],
            full.at[own_rows(ti)],
            ss.at[base + r - 1],
            rs.at[base + r - 1],
            {"tensor": p},
        )
        copy.wait_send()


def start(copies):
    for copy in copies:
        copy.start()


def wait(copies):
    for copy in copies:
        copy.wait()


def head_stack(pieces):
    zero = jnp.zeros((HD, 512), pieces.dtype)
    low = jnp.concatenate([pieces[0:64], pieces[64:128]], axis=1)
    high = jnp.concatenate([pieces[128:192], pieces[192:256]], axis=1)
    top = jnp.concatenate([low, zero], axis=1)
    bottom = jnp.concatenate([zero, high], axis=1)
    return jnp.concatenate([top, bottom], axis=0)


def causal_block():
    keys = lax.broadcasted_iota(jnp.int32, (ROWS, 1024), 0)
    rows = lax.broadcasted_iota(jnp.int32, (ROWS, 1024), 1)
    return keys <= jnp.bitwise_and(rows, ROWS - 1)


class Gather:
    def __init__(self, full, cut, width, ss, rs, base, dp, y, z):
        self.full, self.cut, self.width, self.ss, self.rs, self.base = full, cut, width, ss, rs, base
        self.dp, self.y, self.z = dp, y, z
        self.started = []
        self.a, self.b = pl.ds(0, cut), pl.ds(cut, width - cut)

    def copy(self, ref, k, device):
        return remote(ref, ref, self.ss.at[self.base + k], self.rs.at[self.base + k], device)

    def push(self, ref, k, device):
        copy = self.copy(ref, k, device)
        copy.start()
        self.started.append(copy)

    def seq_id(self, dy, dz):
        return {"seq": lax.rem(self.y + dy, 4) * 4 + lax.rem(self.z + dz, 4)}

    def sibling(self):
        return {"dp": 1 - self.dp}

    def region(self, phase, half, r, dp):
        y, z = lax.rem(self.y + 4 - r, 4), lax.rem(self.z + 4 - r, 4)
        if phase == 0:
            if half == 0:
                return self.full.at[dp, y, self.z, :, self.a]
            return self.full.at[dp, self.y, z, :, self.b]
        if half == 0:
            return self.full.at[dp, :, z, :, self.a]
        return self.full.at[dp, y, :, :, self.b]

    def first(self):
        for r in (1, 3, 2):
            self.push(self.region(0, 0, 0, self.dp), r - 1, self.seq_id(r, 0))
            self.push(self.region(0, 1, 0, self.dp), 3 + r - 1, self.seq_id(0, r))
        self.push(self.full.at[self.dp, self.y, self.z], 12, self.sibling())

    def take(self, phase, rounds):
        here = {"seq": self.y * 4 + self.z}
        for r in rounds:
            for half in (0, 1):
                k = 6 * phase + 3 * half + r - 1
                region = self.region(phase, half, r, self.dp)
                self.copy(region, k, here).wait_recv()
                self.push(region, (13 if phase == 0 else 19) + 3 * half + r - 1, self.sibling())

    def second(self):
        for r in (1, 3, 2):
            self.push(self.region(1, 0, 0, self.dp), 6 + r - 1, self.seq_id(0, r))
            self.push(self.region(1, 1, 0, self.dp), 9 + r - 1, self.seq_id(r, 0))

    def take_sibling(self):
        other = 1 - self.dp
        self.copy(self.full.at[other, self.y, self.z], 12, self.sibling()).wait_recv()
        for phase in (0, 1):
            for r in (1, 3, 2):
                for half in (0, 1):
                    k = (13 if phase == 0 else 19) + 3 * half + r - 1
                    self.copy(self.region(phase, half, r, other), k, self.sibling()).wait_recv()

    def finish(self):
        for copy in self.started:
            copy.wait_send()


class Scatter:
    def __init__(self, grad, landing, cut, width, halves, result, ss, rs, base, dp, y, z):
        self.grad, self.landing, self.cut, self.width, self.halves = grad, landing, cut, width, halves
        self.result, self.ss, self.rs, self.base = result, ss, rs, base
        self.dp, self.y, self.z = dp, y, z
        self.pairs, self.firsts, self.seconds = [], [], []
        self.a, self.b = pl.ds(0, cut), pl.ds(cut, width - cut)

    def copy(self, src, dst, k, device):
        made = remote(src, dst, self.ss.at[self.base + k], self.rs.at[self.base + k], device)
        made.start()
        return made

    def seq_id(self, dy, dz):
        return {"seq": lax.rem(self.y + dy, 4) * 4 + lax.rem(self.z + dz, 4)}

    def pair(self, i):
        rows = pl.ds(2 * i, 2)
        self.pairs.append(
            self.copy(
                self.grad.at[1 - self.dp, rows], self.landing.at[rows], 12 + i, {"dp": 1 - self.dp}
            )
        )

    def first(self):
        wait(self.pairs)

        def add(i, carry):
            y, z = lax.div(i, 4), lax.rem(i, 4)
            self.grad[self.dp, y, z] = (
                self.grad[self.dp, y, z].astype(f32) + self.landing[y, z].astype(f32)
            ).astype(bf16)
            return carry

        lax.fori_loop(0, 16, add, 0)
        for r in (2, 1, 3):
            y, z = lax.rem(self.y + r, 4), lax.rem(self.z + r, 4)
            self.firsts.append(
                self.copy(
                    self.grad.at[self.dp, :, z, :, self.a],
                    self.halves[0][0].at[r - 1],
                    r - 1,
                    self.seq_id(0, r),
                )
            )
            self.firsts.append(
                self.copy(
                    self.grad.at[self.dp, y, :, :, self.b],
                    self.halves[1][0].at[r - 1],
                    3 + r - 1,
                    self.seq_id(r, 0),
                )
            )

    def second(self):
        wait(self.firsts)
        for m in (0, 1):
            arrived, kept, last = self.halves[m]

            def add(i, carry):
                if m == 0:
                    mine = self.grad[self.dp, i, self.z, :, 0 : self.cut]
                else:
                    mine = self.grad[self.dp, self.y, i, :, self.cut : self.width]
                summed = mine.astype(f32)
                for r in range(3):
                    summed += arrived[r, i].astype(f32)
                kept[i] = summed.astype(bf16)
                return carry

            lax.fori_loop(0, 4, add, 0)
            for r in (2, 1, 3):
                to = lax.rem((self.y if m == 0 else self.z) + r, 4)
                target = self.seq_id(r, 0) if m == 0 else self.seq_id(0, r)
                self.seconds.append(
                    self.copy(kept.at[to], last.at[r - 1], 6 + 3 * m + r - 1, target)
                )

    def finish(self):
        wait(self.seconds)
        for m in (0, 1):
            arrived, kept, last = self.halves[m]
            summed = kept[self.y if m == 0 else self.z].astype(f32)
            for r in range(3):
                summed += last[r].astype(f32)
            if m == 0:
                self.result[:, 0 : self.cut] = summed
            else:
                self.result[:, self.cut : self.width] = summed


def block_kernel(
    x, dy, qw, kvw, ow, guw, dw, ng, hg, base_cs, block_cs,
    out, ig16, fa, ff, norm_grad, head_grad,
    wa, wf, ga, gf, ra, rf, a_in0, a_in1, f_in0, f_in1, a_k0, a_k1, f_k0, f_k1, a_l0, a_l1, f_l0, f_l1,
    h1, h1t, qkt, qpad, q_nat, kv, o16, lse, h2, hres, gains, acc, delta, dot_pad, do_nat, dq, dkv, dkv_in,
    z_, dg, du, dyt, h2t, dres16, dres, part_a, land_a, part_d, land_d, part_o, land_o, part_h, land_h,
    small, stage, small_in, turned,
    wss, wrs, gss, grs, kss, krs, bss, brs, ts, tr, mss, mrs,
):
    dp = lax.axis_index("dp")
    si = lax.axis_index("seq")
    ti = lax.axis_index("tensor")
    y, z = lax.div(si, 4), lax.rem(si, 4)
    rows = own_rows(ti)
    sibling = {"dp": 1 - dp}

    barrier = pltpu.get_barrier_semaphore()
    for r in (1, 2, 3):
        pl.semaphore_signal(
            barrier, inc=1, device_id={"tensor": lax.rem(ti + r, 4)}, device_id_type=MESH
        )
    pl.semaphore_signal(barrier, inc=1, device_id=sibling, device_id_type=MESH)

    def greet(r, carry):
        pl.semaphore_signal(
            barrier, inc=1, device_id={"seq": lax.rem(si + r, 16)}, device_id_type=MESH
        )
        return carry

    lax.fori_loop(1, 16, greet, 0)

    wa[dp, y, z, :, 0:256] = qw[...].astype(bf16)
    wa[dp, y, z, :, 256:384] = kvw[:, 0, :].astype(bf16)
    wa[dp, y, z, :, 384:512] = kvw[:, 1, :].astype(bf16)
    wa[dp, y, z, :, 512:768] = ow[...].astype(bf16)
    line = lax.broadcasted_iota(jnp.int32, (128, 32), 0)
    wa[dp, y, z, :, 768:896] = jnp.where(
        line == 0, ng[0:1], jnp.where(line == 1, ng[1:2], 0.0)
    ).T.astype(bf16)
    pl.semaphore_wait(barrier, 19)
    weights_a = Gather(wa, SPLIT_A, CA, wss, wrs, 0, dp, y, z)
    weights_f = Gather(wf, SPLIT_F, CF, wss, wrs, 25, dp, y, z)
    weights_a.first()
    wf[dp, y, z, :, 0:FFC] = guw[:, 0, :].astype(bf16)
    wf[dp, y, z, :, FFC : 2 * FFC] = guw[:, 1, :].astype(bf16)
    wf[dp, y, z, :, 2 * FFC : 3 * FFC] = dw[...].astype(bf16)
    weights_a.take(0, (1, 3, 2))
    weights_a.second()
    weights_f.first()

    x32 = x[...].astype(f32)
    h1_scale = x32 * lax.rsqrt(jnp.mean(x32 * x32, axis=-1, keepdims=True) + norm_eps)
    dyt[...] = transposed(dy[...], bf16)
    lanes = lax.broadcasted_iota(jnp.int32, (64, 128), 1)
    turn = jnp.sum(jnp.where(lanes == si, block_cs[...], 0.0), axis=1, keepdims=True)
    cos_b, sin_b = turn[0:32], turn[32:64]
    cos_t, sin_t = base_cs[0:32], base_cs[32:64]
    cosine = cos_t * cos_b - sin_t * sin_b
    sine = sin_t * cos_b + cos_t * sin_b
    square = lax.broadcasted_iota(jnp.int32, (64, 64), 0) == lax.broadcasted_iota(
        jnp.int32, (64, 64), 1
    )
    q_gain = jnp.sum(jnp.where(square, hg[0:1], 0.0), axis=1, keepdims=True)
    k_gain = jnp.sum(jnp.where(square, hg[1:2], 0.0), axis=1, keepdims=True)

    weights_a.take(1, (1, 3, 2))
    weights_a.take_sibling()

    def columns_a(lo, hi):
        return wa[:, :, :, :, lo:hi].reshape(1024, hi - lo)

    gains[...] = columns_a(768, 896).astype(f32).T[0:8]
    h1[...] = (h1_scale * gains[0:1]).astype(bf16)
    qkv = dot_nn(h1[...], columns_a(0, 512))
    qk = qkv[:, 0:384].T
    qkt[...] = qk
    rotated = []
    for h in (4, 5, 0, 1, 2, 3):
        one = qk[64 * h : 64 * h + 64]
        hat = one * lax.rsqrt(jnp.mean(one * one, axis=0, keepdims=True) + norm_eps)
        scaled = hat * (q_gain if h < 4 else k_gain)
        a, b = scaled[0:32], scaled[32:64]
        rotated += [a * cosine - b * sine, b * cosine + a * sine]
    kv[si, :, 0:128] = jnp.concatenate(rotated[0:4], axis=0).T.astype(bf16)
    kv[si, :, 128:256] = qkv[:, 384:512].astype(bf16)

    def send_kv(r):
        return remote(kv.at[si], kv.at[si], kss.at[r], krs.at[r], {"seq": si + r})

    def send_one(r, carry):
        send_kv(r).start()
        return carry

    lax.fori_loop(1, 16 - si, send_one, 0)
    qpad[...] = head_stack(jnp.concatenate(rotated[4:12], axis=0).astype(bf16))
    ones = jnp.ones((16, ROWS), bf16)
    weights_f.take(0, (1, 3, 2))

    def visit_forward(block, diagonal):
        k16 = kv[block, :, 0:128]
        p = jnp.exp2(dot_nn(k16, qpad[...]) * (SCALE * LOG2E))
        if diagonal:
            p = jnp.where(causal_block(), p, 0.0)
        p16 = p.astype(bf16)
        vt = transposed(kv[block, :, 128:256], bf16)
        for j in range(2):
            lhs = jnp.concatenate([vt[64 * j : 64 * j + 64], ones], axis=0)
            product = dot_nn(lhs, p16[:, 512 * j : 512 * j + 512])
            if diagonal:
                acc[j] = product
            else:
                acc[j] += product

    visit_forward(si, True)

    def later_forward(r, carry):
        block = si - r
        remote(kv.at[block], kv.at[block], kss.at[r], krs.at[r], {"seq": block}).wait_recv()
        visit_forward(block, False)
        return carry

    lax.fori_loop(1, si + 1, later_forward, 0)
    weights_f.second()
    pieces = []
    for j in range(2):
        total = acc[j, 64:65]
        piece = acc[j, 0:64] / total
        lse[j : j + 1] = jnp.log(total) * LOG2E
        pieces += [piece[:, 0:256], piece[:, 256:512]]
    o16[...] = jnp.concatenate(pieces, axis=0).T.astype(bf16)
    part_a[...] = dot_nt(o16[...], columns_a(512, 768)).astype(bf16)
    copies = scatter_copies(part_a, land_a, ts, tr, 0, ti)
    start(copies)
    h1t[...] = transposed(h1[...], bf16)
    q_nat[...] = transposed(qpad[...], bf16)
    wait(copies)
    mid = x[rows].astype(f32) + part_a[rows].astype(f32)
    for r in range(3):
        mid += land_a[r].astype(f32)
    hres[...] = mid
    inverse = lax.rsqrt(jnp.mean(mid * mid, axis=-1, keepdims=True) + norm_eps)
    h2[rows] = (mid * inverse * gains[1:2]).astype(bf16)
    start(gather_copies(h2, ts, tr, 3, ti))
    weights_f.take(1, (1, 3, 2))
    gather_waits(h2, ts, tr, 3, ti)
    h2t[...] = transposed(h2[...], bf16)
    weights_f.take_sibling()

    width = 384

    def columns_f(at, count):
        return wf[:, :, :, :, pl.ds(at, count)].reshape(1024, count)

    def hidden(c, carry):
        at = pl.multiple_of(c * width, 128)
        gate = dot_nn(h2[...], columns_f(at, width))
        up = dot_nn(h2[...], columns_f(at + FFC, width))
        dz = dot_nn(dy[...], columns_f(at + 2 * FFC, width))
        sigma = jax.nn.sigmoid(gate)
        silu = gate * sigma
        z_[:, pl.ds(at, width)] = (silu * up).astype(bf16)
        dg[:, pl.ds(at, width)] = (dz * up * sigma * (1.0 + gate * (1.0 - sigma))).astype(bf16)
        du[:, pl.ds(at, width)] = (dz * silu).astype(bf16)
        return carry

    lax.fori_loop(0, 3, hidden, 0)

    def rows_f(n, lo, hi):
        return wf[lax.div(n, 2), pl.ds(lax.rem(n, 2) * 2, 2), :, :, lo:hi].reshape(256, hi - lo)

    def back_d(n, carry):
        at = pl.ds(pl.multiple_of(n * 256, 256), 256)
        part_d[:, at] = (
            dot_nt(dg[...], rows_f(n, 0, FFC)) + dot_nt(du[...], rows_f(n, FFC, 2 * FFC))
        ).astype(bf16)
        return carry

    lax.fori_loop(0, 4, back_d, 0)
    copies_d = scatter_copies(part_d, land_d, ts, tr, 6, ti)
    start(copies_d)
    halves_a = ((a_in0, a_k0, a_l0), (a_in1, a_k1, a_l1))
    halves_f = ((f_in0, f_k0, f_l0), (f_in1, f_k1, f_l1))
    grads_a = Scatter(ga, ra, SPLIT_G, CG, halves_a, fa, gss, grs, 0, dp, y, z)
    grads_f = Scatter(gf, rf, SPLIT_F, CF, halves_f, ff, gss, grs, 14, dp, y, z)

    def grad_rows(owner, i):
        at = pl.ds(pl.multiple_of((2 * owner + i) * 256, 256), 256)
        for k, (left, right) in enumerate(((h2t, dg), (h2t, du), (dyt, z_))):
            value = dot_nn(left[at], right[...]).astype(bf16)
            gf[owner, 2 * i : 2 * i + 2, :, :, k * FFC : (k + 1) * FFC] = value.reshape(
                2, 4, 32, FFC
            )

    for i in range(2):
        grad_rows(1 - dp, i)
        grads_f.pair(i)
    for i in range(2):
        grad_rows(dp, i)

    def back_o(n, carry):
        at = pl.ds(pl.multiple_of(n * 256, 256), 256)
        part_o[:, at] = dot_nt(z_[...], rows_f(n, 2 * FFC, 3 * FFC)).astype(bf16)
        return carry

    lax.fori_loop(0, 4, back_o, 0)
    wait(copies_d)
    dh2 = part_d[rows].astype(f32)
    for r in range(3):
        dh2 += land_d[r].astype(f32)
    mid = hres[...]
    inverse = lax.rsqrt(jnp.mean(mid * mid, axis=-1, keepdims=True) + norm_eps)
    normed = mid * inverse
    scaled = dh2 * gains[1:2]
    inner = jnp.mean(scaled * normed, axis=-1, keepdims=True)
    grad = dy[rows].astype(f32) + inverse * (scaled - normed * inner)
    dres[...] = grad
    dres16[rows] = grad.astype(bf16)
    start(gather_copies(dres16, ts, tr, 9, ti))
    norm_two = jnp.sum(dh2 * normed, axis=0, keepdims=True)
    grads_f.first()
    copies_o = scatter_copies(part_o, land_o, ts, tr, 12, ti)
    gather_waits(dres16, ts, tr, 9, ti)
    start(copies_o)

    do_t = transposed(dot_nn(dres16[...], columns_a(512, 768)).astype(bf16), f32)
    products = do_t * transposed(o16[...], f32)
    sums = [jnp.sum(products[64 * h : 64 * h + 64], axis=0, keepdims=True) for h in range(4)]
    delta[...] = jnp.concatenate(sums, axis=1)
    dot_pad[...] = head_stack(do_t.astype(bf16))
    do_nat[...] = transposed(dot_pad[...], bf16)

    def visit_backward(block, diagonal):
        k16 = kv[block, :, 0:128]
        kt = transposed(k16, bf16)
        shift = jnp.concatenate([lse[0:1], lse[1:2]], axis=1)
        p = jnp.exp2(dot_nn(k16, qpad[...]) * (SCALE * LOG2E) - shift)
        if diagonal:
            p = jnp.where(causal_block(), p, 0.0)
        dprob = dot_nn(kv[block, :, 128:256], dot_pad[...])
        ds16 = (p * (dprob - delta[...])).astype(bf16)
        dkv[block, :, 0:128] = (dot_nn(ds16, q_nat[...]) * SCALE).astype(bf16)
        dkv[block, :, 128:256] = dot_nn(p.astype(bf16), do_nat[...]).astype(bf16)
        for j in range(2):
            product = dot_nn(kt[64 * j : 64 * j + 64], ds16[:, 512 * j : 512 * j + 512])
            if diagonal:
                dq[j] = product
            else:
                dq[j] += product

    visit_backward(si, True)

    def send_dkv(r):
        return remote(dkv.at[si - r], dkv_in.at[r], bss.at[r], brs.at[r], {"seq": si - r})

    def later_backward(r, carry):
        visit_backward(si - r, False)
        send_dkv(r).start()
        return carry

    lax.fori_loop(1, si + 1, later_backward, 0)

    wait(copies_o)
    ffn = part_o[rows].astype(f32)
    for r in range(3):
        ffn += land_o[r].astype(f32)
    out[rows] = (hres[...] + ffn).astype(bf16)
    start(gather_copies(out, ts, tr, 15, ti))
    hats, inverses = [], []
    for h in range(6):
        one = qkt[64 * h : 64 * h + 64]
        inverse = lax.rsqrt(jnp.mean(one * one, axis=0, keepdims=True) + norm_eps)
        inverses.append(inverse)
        hats.append(one * inverse)

    def head_back(gradient, h):
        a, b = gradient[0:32], gradient[32:64]
        normed = jnp.concatenate([a * cosine + b * sine, b * cosine - a * sine], axis=0)
        scaled = normed * (q_gain if h < 4 else k_gain)
        inner = jnp.mean(scaled * hats[h], axis=0, keepdims=True)
        return inverses[h] * (scaled - hats[h] * inner), normed * hats[h]

    results, q_products = [], 0.0
    for h in range(4):
        piece = dq[h // 2, :, 256 * (h % 2) : 256 * (h % 2) + 256] * SCALE
        result, product = head_back(piece, h)
        results.append(result)
        q_products = q_products + product
    grad_o = dot_nn(transposed(dres16[...], bf16), o16[...]).astype(bf16)
    ga[:, :, :, :, 512:768] = grad_o.reshape(2, 4, 4, 32, 256)

    def receive(r, total):
        remote(dkv.at[si], dkv_in.at[r], bss.at[r], brs.at[r], {"seq": si}).wait_recv()
        return total + dkv_in[r].astype(f32)

    total = lax.fori_loop(1, 16 - si, receive, dkv[si].astype(f32))
    dkt = total[:, 0:128].T
    k_products = 0.0
    for h in range(2):
        result, product = head_back(dkt[64 * h : 64 * h + 64], 4 + h)
        results.append(result)
        k_products = k_products + product
    dqk = jnp.concatenate(results, axis=0).T.astype(bf16)
    dqkv = jnp.concatenate([dqk, total[:, 128:256].astype(bf16)], axis=1)
    grad_qkv = dot_nn(h1t[...], dqkv).astype(bf16)
    ga[:, :, :, :, 0:512] = grad_qkv.reshape(2, 4, 4, 32, 512)
    for i in range(2):
        grads_a.pair(i)
    part_h[...] = dot_nt(dqkv, columns_a(0, 512)).astype(bf16)
    copies_h = scatter_copies(part_h, land_h, ts, tr, 18, ti)
    start(copies_h)
    blank = jnp.zeros((1, 960), f32)
    head_rows = [
        jnp.concatenate([jnp.sum(q_products.T, axis=0, keepdims=True), blank], axis=1),
        jnp.concatenate([jnp.sum(k_products.T, axis=0, keepdims=True), blank], axis=1),
    ]
    grads_f.second()
    grads_a.first()
    wait(copies_h)
    dh1 = part_h[rows].astype(f32)
    for r in range(3):
        dh1 += land_h[r].astype(f32)
    own_x = x[rows].astype(f32)
    inverse = lax.rsqrt(jnp.mean(own_x * own_x, axis=-1, keepdims=True) + norm_eps)
    normed = own_x * inverse
    norm_one = jnp.sum(dh1 * normed, axis=0, keepdims=True)
    small[0] = jnp.concatenate([norm_one, norm_two] + head_rows + [jnp.zeros((4, 1024), f32)], axis=0)
    small_x = [
        remote(
            small.at[0], small.at[r], mss.at[r - 1], mrs.at[r - 1], {"tensor": lax.rem(ti + r, 4)}
        )
        for r in (1, 2, 3)
    ]
    start(small_x)
    scaled = dh1 * gains[0:1]
    inner = jnp.mean(scaled * normed, axis=-1, keepdims=True)
    ig16[rows] = (dres[...] + inverse * (scaled - normed * inner)).astype(bf16)
    start(gather_copies(ig16, ts, tr, 21, ti))
    wait(small_x)
    stage[0] = small[0] + small[1] + small[2] + small[3]
    small_c = [remote(stage.at[0], small_in.at[0], mss.at[3], mrs.at[3], sibling)]
    start(small_c)
    grads_a.second()
    wait(small_c)
    stage[1] = stage[0] + small_in[0]
    small_z = [
        remote(
            stage.at[1], small_in.at[r], mss.at[3 + r], mrs.at[3 + r],
            {"seq": y * 4 + lax.rem(z + r, 4)},
        )
        for r in (1, 2, 3)
    ]
    start(small_z)
    grads_f.finish()
    wait(small_z)
    stage[2] = stage[1] + small_in[1] + small_in[2] + small_in[3]
    small_y = [
        remote(
            stage.at[2], small_in.at[3 + r], mss.at[6 + r], mrs.at[6 + r],
            {"seq": lax.rem(y + r, 4) * 4 + z},
        )
        for r in (1, 2, 3)
    ]
    start(small_y)
    grads_a.finish()
    wait(small_y)
    summed = stage[2] + small_in[4] + small_in[5] + small_in[6]
    head_grad[...] = summed[2:4, 0:64]
    turned[...] = jnp.concatenate([summed, jnp.zeros((120, 1024), f32)], axis=0).T
    mine = turned[pl.ds(pl.multiple_of((dp * 16 + si) * 32, 32), 32), :]
    norm_grad[...] = mine.T[0:2]

    def kv_done(r, carry):
        send_kv(r).wait_send()
        return carry

    lax.fori_loop(1, 16 - si, kv_done, 0)

    def dkv_done(r, carry):
        send_dkv(r).wait_send()
        return carry

    lax.fori_loop(1, si + 1, dkv_done, 0)
    weights_a.finish()
    weights_f.finish()
    gather_waits(out, ts, tr, 15, ti)
    gather_waits(ig16, ts, tr, 21, ti)


def block_step(*operands):
    def b(*shape):
        return pltpu.VMEM(shape, bf16)

    def f(*shape):
        return pltpu.VMEM(shape, f32)

    def s(count):
        return pltpu.SemaphoreType.DMA((count,))

    rest_a, rest_f = CG - SPLIT_G, CF - SPLIT_F
    return pl.pallas_call(
        block_kernel,
        out_shape=(
            jax.ShapeDtypeStruct((256, 1024), bf16),
            jax.ShapeDtypeStruct((256, 1024), bf16),
            jax.ShapeDtypeStruct((32, CG), f32),
            jax.ShapeDtypeStruct((32, CF), f32),
            jax.ShapeDtypeStruct((2, 32), f32),
            jax.ShapeDtypeStruct((2, 64), f32),
        ),
        in_specs=[VMEM] * len(operands),
        out_specs=(VMEM,) * 6,
        scratch_shapes=[
            b(2, 4, 4, 32, CA), b(2, 4, 4, 32, CF), b(2, 4, 4, 32, CG), b(2, 4, 4, 32, CF),
            b(4, 4, 32, CG), b(4, 4, 32, CF),
            b(3, 4, 32, SPLIT_G), b(3, 4, 32, rest_a), b(3, 4, 32, SPLIT_F), b(3, 4, 32, rest_f),
            b(4, 32, SPLIT_G), b(4, 32, rest_a), b(4, 32, SPLIT_F), b(4, 32, rest_f),
            b(3, 32, SPLIT_G), b(3, 32, rest_a), b(3, 32, SPLIT_F), b(3, 32, rest_f),
            b(256, 1024), b(1024, 256), f(384, 256), b(128, 1024), b(1024, 128), b(16, 256, 256),
            b(256, 256), f(2, 512), b(256, 1024), f(64, 1024), f(8, 1024), f(2, 80, 512), f(1, 1024),
            b(128, 1024), b(1024, 128), f(2, 64, 512), b(16, 256, 256), b(16, 256, 256),
            b(256, FFC), b(256, FFC), b(256, FFC), b(1024, 256), b(1024, 256), b(256, 1024), f(64, 1024),
            b(256, 1024), b(3, 64, 1024), b(256, 1024), b(3, 64, 1024),
            b(256, 1024), b(3, 64, 1024), b(256, 1024), b(3, 64, 1024),
            f(4, 8, 1024), f(3, 8, 1024), f(7, 8, 1024), f(1024, 128),
            s(50), s(50), s(28), s(28), s(16), s(16), s(16), s(16), s(24), s(24), s(10), s(10),
        ],
        compiler_params=params(1, 62),
        name="block_step",
    )(*operands)


def adamw(weight, momentum, variance, gradient, decay):
    first = beta_one * momentum + (1.0 - beta_one) * gradient
    second = beta_two * variance + (1.0 - beta_two) * gradient * gradient
    first_fixed = first / (1.0 - beta_one**adam_count)
    second_fixed = second / (1.0 - beta_two**adam_count)
    direction = first_fixed / (jnp.sqrt(second_fixed) + adam_eps) + decay * weight
    return (direction, first, second)


def adam_kernel(*refs):
    fa, ff, norm_grad, head_grad = refs[0:4]
    weights, momenta, variances = refs[4:11], refs[11:18], refs[18:25]
    grads, directions, firsts, seconds = refs[25:32], refs[32:39], refs[39:46], refs[46:53]
    grads[0][...] = fa[:, 0:256]
    grads[1][:, 0, :] = fa[:, 256:384]
    grads[1][:, 1, :] = fa[:, 384:512]
    grads[2][...] = fa[:, 512:768]
    grads[3][:, 0, :] = ff[:, 0:FFC]
    grads[3][:, 1, :] = ff[:, FFC : 2 * FFC]
    grads[4][...] = ff[:, 2 * FFC : 3 * FFC]
    grads[5][...] = norm_grad[...]
    grads[6][...] = head_grad[...]
    for n in range(7):
        direction, first, second = adamw(
            weights[n][...],
            momenta[n][...],
            variances[n][...],
            grads[n][...],
            decay_rate if n < 5 else 0.0,
        )
        directions[n][...] = direction
        firsts[n][...] = first
        seconds[n][...] = second


def adam_step(found, weights, momenta, variances):
    shapes = tuple(jax.ShapeDtypeStruct(w.shape, f32) for w in weights)
    return pl.pallas_call(
        adam_kernel,
        out_shape=shapes * 4,
        in_specs=[VMEM] * 25,
        out_specs=(VMEM,) * 28,
        compiler_params=pltpu.CompilerParams(vmem_limit_bytes=40 * 1024 * 1024),
        name="adam_step",
    )(*found, *weights, *momenta, *variances)


def rope_constants():
    frequency = rope_base ** (-(np.arange(HD // 2, dtype=np.float64) * 2.0) / HD)
    base = frequency[:, None] * np.arange(ROWS)[None, :]
    block = frequency[:, None] * (ROWS * np.arange(128) * (np.arange(128) < 16))[None, :]
    return tuple(
        np.concatenate([np.cos(a), np.sin(a)], axis=0).astype(np.float32) for a in (base, block)
    )


def body(
    block_input,
    upstream_grad,
    query_weight,
    key_value_weight,
    output_weight,
    gateup_weight,
    down_weight,
    norm_gains,
    head_norm_gains,
    query_momentum,
    query_variance,
    key_value_momentum,
    key_value_variance,
    output_momentum,
    output_variance,
    gateup_momentum,
    gateup_variance,
    down_momentum,
    down_variance,
    norm_momentum,
    norm_variance,
    head_momentum,
    head_variance,
):
    base_cs, block_cs = rope_constants()
    weights = (
        query_weight, key_value_weight, output_weight, gateup_weight, down_weight, norm_gains.T,
        head_norm_gains,
    )
    momenta = (
        query_momentum, key_value_momentum, output_momentum, gateup_momentum, down_momentum,
        norm_momentum.T, head_momentum,
    )
    variances = (
        query_variance, key_value_variance, output_variance, gateup_variance, down_variance,
        norm_variance.T, head_variance,
    )
    out, ig16, *found = block_step(
        block_input[0], upstream_grad[0], *weights, jnp.asarray(base_cs), jnp.asarray(block_cs)
    )
    results = adam_step(found, weights, momenta, variances)
    grads, directions, firsts, seconds = (
        [v.T if n == 5 else v for n, v in enumerate(results[7 * i : 7 * i + 7])] for i in range(4)
    )
    moments = [v for pair in zip(firsts, seconds) for v in pair]
    return (out[None], ig16.astype(f32)[None], *grads, *directions, *moments)


def solution(mesh):
    in_specs = (
        P("dp", "seq", None),
        P("dp", "seq", None),
        P(("dp", "seq"), "tensor"),
        P(("dp", "seq"), None, "tensor"),
        P(("dp", "seq"), "tensor"),
        P(("dp", "seq"), None, "tensor"),
        P(("dp", "seq"), "tensor"),
        P(("dp", "seq"), None),
        P(),
        P(("dp", "seq"), "tensor"),
        P(("dp", "seq"), "tensor"),
        P(("dp", "seq"), None, "tensor"),
        P(("dp", "seq"), None, "tensor"),
        P(("dp", "seq"), "tensor"),
        P(("dp", "seq"), "tensor"),
        P(("dp", "seq"), None, "tensor"),
        P(("dp", "seq"), None, "tensor"),
        P(("dp", "seq"), "tensor"),
        P(("dp", "seq"), "tensor"),
        P(("dp", "seq"), None),
        P(("dp", "seq"), None),
        P(),
        P(),
    )
    out_specs = (
        P("dp", "seq", None),
        P("dp", "seq", None),
        P(("dp", "seq"), "tensor"),
        P(("dp", "seq"), None, "tensor"),
        P(("dp", "seq"), "tensor"),
        P(("dp", "seq"), None, "tensor"),
        P(("dp", "seq"), "tensor"),
        P(("dp", "seq"), None),
        P(),
        P(("dp", "seq"), "tensor"),
        P(("dp", "seq"), None, "tensor"),
        P(("dp", "seq"), "tensor"),
        P(("dp", "seq"), None, "tensor"),
        P(("dp", "seq"), "tensor"),
        P(("dp", "seq"), None),
        P(),
        P(("dp", "seq"), "tensor"),
        P(("dp", "seq"), "tensor"),
        P(("dp", "seq"), None, "tensor"),
        P(("dp", "seq"), None, "tensor"),
        P(("dp", "seq"), "tensor"),
        P(("dp", "seq"), "tensor"),
        P(("dp", "seq"), None, "tensor"),
        P(("dp", "seq"), None, "tensor"),
        P(("dp", "seq"), "tensor"),
        P(("dp", "seq"), "tensor"),
        P(("dp", "seq"), None),
        P(("dp", "seq"), None),
        P(),
        P(),
    )
    return jax.shard_map(body, mesh=mesh, in_specs=in_specs, out_specs=out_specs, check_vma=False)
```

time: 279 us -> 182 us (0.65)
  Pallas kernels: 254 us -> 176 us
  local copies, waits for them, and re-layouts: 14.5 us -> 3.27 us
  other arithmetic: 8.24 us -> 1.08 us
    pallas_call x5 -> x2, Pallas kernels: 254 us -> 176 us  [the longest x1 174 us: block_step(): pl.pallas_call(block_kernel, out_shape=(jax.ShapeDtypeStruct((256, 1024),...]
    unnamed x67 -> x55, local copies, waits for them, and re-layouts: 13.3 us -> 3.27 us
    add x6 -> x0, other arithmetic: 3.48 us -> none  [adamw(): first_fixed / (jnp.sqrt(second_fixed) + adam_eps) + decay * weight]
where the time goes in v2:
time: 182 us; the launch traced here: 181 us
  Pallas kernels  176 us (97%)
  local copies, waits for them, and re-layouts  3.27 us (2%)
    pallas_call x1, Pallas kernels, block_step(): pl.pallas_call(block_kernel, out_shape=(jax.ShapeDtypeStruct((256, 1024),...  174 us

profile of v2, /device:TPU:0, one launch (start us, length us, event | category | flops | bytes accessed | tf_op | source)
XLA Modules:
  0.0 181.2 jit_solution(3800127469780742975)
XLA Ops:
  0.7 0.0 copy-start
  0.7 0.0 copy-start.1
  0.7 0.0 copy-start.3
  0.7 0.0 copy-start.4
  0.7 0.0 copy-start.5
  0.7 0.0 copy-start.6
  0.7 0.0 copy-start.7
  0.7 0.0 copy-start.8
  0.8 0.0 copy-start.9
  0.8 0.0 copy-start.11
  0.8 0.0 copy-start.12
  0.8 0.0 copy-start.13
  0.8 0.0 copy-start.14
  0.8 0.0 copy-start.15
  0.8 0.0 copy-start.16
  0.8 0.0 copy-start.18
  0.8 0.0 copy-start.19
  0.8 0.0 copy-start.20
  0.9 0.0 copy-start.21
  0.9 174.1 %block_step.1 = (bf16[256,1024]{1,0:T(8,128)(2,1)}, bf16[256,1024]{1,0:T(8,128)(2,1)}, f32[32,768]{1,0:T(8,128)}, f32[32,3456]{1,0:T(8,128)}, f32[2,32]{1,0:T(2,128)}, /*index=5*/f32[2,64]{1,0:T(2,128)}) custom-call(bf16[256,1024]{1,0:T(8,128)(2,1)} %bitcast.17, bf16[256,1024]{1,0:T(8,128)(2,1)} %bitcast.18, f32[32,256]{1,0:T(8,128)} %refs_4_.1, ...), custom_call_target="tpu_custom_call" | custom-call | tf_op jit(solution)/shard_map/block_step/pallas_call | solution.py:710
  175.0 0.0 copy-start.17
  175.2 0.4 copy-done.23
  175.6 0.0 copy-done.24
  175.6 0.0 copy-done.17
  175.7 1.0 copy-done.2
  176.7 0.9 copy-done.10
  177.6 1.8 adam_step.1
  179.3 0.0 copy-done.25
  179.3 0.0 copy-start.26
  179.3 1.1 bitcast_convert_fusion
  180.4 0.0 copy-done.26
  180.4 0.8 copy.56
  (26 shorter events, 0.1 us)
Async XLA Ops:
  0.7 174.3 %copy-start = (f32[32,2,1152]{2,1,0:T(2,128)S(1)}, f32[32,2,1152]{2,1,0:T(2,128)}, u32[]{:S(2)}) copy-start(f32[32,2,1152]{2,1,0:T(2,128)} %refs_7_.1) | copy-start | bytes 884740
  0.7 174.3 %copy-start.1 = (f32[32,1152]{1,0:T(8,128)S(1)}, f32[32,1152]{1,0:T(8,128)}, u32[]{:S(2)}) copy-start(f32[32,1152]{1,0:T(8,128)} %refs_8_.1) | copy-start | bytes 442372
  0.7 174.3 %copy-start.3 = (f32[32,2,1152]{2,1,0:T(2,128)S(1)}, f32[32,2,1152]{2,1,0:T(2,128)}, u32[]{:S(2)}) copy-start(f32[32,2,1152]{2,1,0:T(2,128)} %refs_14_.1) | copy-start | bytes 884740
  0.7 174.3 %copy-start.4 = (f32[32,2,1152]{2,1,0:T(2,128)S(1)}, f32[32,2,1152]{2,1,0:T(2,128)}, u32[]{:S(2)}) copy-start(f32[32,2,1152]{2,1,0:T(2,128)} %refs_21_.1) | copy-start | bytes 884740
  0.7 174.3 %copy-start.5 = (f32[32,1152]{1,0:T(8,128)S(1)}, f32[32,1152]{1,0:T(8,128)}, u32[]{:S(2)}) copy-start(f32[32,1152]{1,0:T(8,128)} %refs_15_.1) | copy-start | bytes 442372
  0.7 174.3 %copy-start.6 = (f32[32,1152]{1,0:T(8,128)S(1)}, f32[32,1152]{1,0:T(8,128)}, u32[]{:S(2)}) copy-start(f32[32,1152]{1,0:T(8,128)} %refs_22_.1) | copy-start | bytes 442372
  0.7 174.3 %copy-start.7 = (f32[32,256]{1,0:T(8,128)S(1)}, f32[32,256]{1,0:T(8,128)}, u32[]{:S(2)}) copy-start(f32[32,256]{1,0:T(8,128)} %refs_4_.1) | copy-start | bytes 98308
  0.7 174.3 %copy-start.8 = (f32[32,2,128]{2,1,0:T(2,128)S(1)}, f32[32,2,128]{2,1,0:T(2,128)}, u32[]{:S(2)}) copy-start(f32[32,2,128]{2,1,0:T(2,128)} %refs_5_.1) | copy-start | bytes 98308
  0.8 174.3 %copy-start.9 = (f32[32,256]{1,0:T(8,128)S(1)}, f32[32,256]{1,0:T(8,128)}, u32[]{:S(2)}) copy-start(f32[32,256]{1,0:T(8,128)} %refs_6_.1) | copy-start | bytes 98308
  0.8 174.3 %copy-start.11 = (f32[32,256]{1,0:T(8,128)S(1)}, f32[32,256]{1,0:T(8,128)}, u32[]{:S(2)}) copy-start(f32[32,256]{1,0:T(8,128)} %refs_11_.1) | copy-start | bytes 98308
  0.8 174.3 %copy-start.12 = (f32[32,2,128]{2,1,0:T(2,128)S(1)}, f32[32,2,128]{2,1,0:T(2,128)}, u32[]{:S(2)}) copy-start(f32[32,2,128]{2,1,0:T(2,128)} %refs_12_.1) | copy-start | bytes 98308
  0.8 174.3 %copy-start.13 = (f32[32,256]{1,0:T(8,128)S(1)}, f32[32,256]{1,0:T(8,128)}, u32[]{:S(2)}) copy-start(f32[32,256]{1,0:T(8,128)} %refs_13_.1) | copy-start | bytes 98308
  0.8 174.3 %copy-start.14 = (f32[32,256]{1,0:T(8,128)S(1)}, f32[32,256]{1,0:T(8,128)}, u32[]{:S(2)}) copy-start(f32[32,256]{1,0:T(8,128)} %refs_18_.1) | copy-start | bytes 98308
  0.8 174.3 %copy-start.15 = (f32[32,2,128]{2,1,0:T(2,128)S(1)}, f32[32,2,128]{2,1,0:T(2,128)}, u32[]{:S(2)}) copy-start(f32[32,2,128]{2,1,0:T(2,128)} %refs_19_.1) | copy-start | bytes 98308
  0.8 174.3 %copy-start.16 = (f32[32,256]{1,0:T(8,128)S(1)}, f32[32,256]{1,0:T(8,128)}, u32[]{:S(2)}) copy-start(f32[32,256]{1,0:T(8,128)} %refs_20_.1) | copy-start | bytes 98308
  0.8 174.3 %copy-start.18 = (f32[2,64]{1,0:T(2,128)S(1)}, f32[2,64]{1,0:T(2,128)}, u32[]{:S(2)}) copy-start(f32[2,64]{1,0:T(2,128)} %refs_10_.1) | copy-start | bytes 1540
  0.8 174.3 %copy-start.19 = (f32[32,2]{0,1:T(2,128)S(1)}, f32[32,2]{0,1:T(2,128)}, u32[]{:S(2)}) copy-start(f32[32,2]{0,1:T(2,128)} %param.44) | copy-start | bytes 772
  0.8 174.3 %copy-start.20 = (f32[2,64]{1,0:T(2,128)S(1)}, f32[2,64]{1,0:T(2,128)}, u32[]{:S(2)}) copy-start(f32[2,64]{1,0:T(2,128)} %refs_17_.1) | copy-start | bytes 1540
  0.9 174.3 %copy-start.21 = (f32[32,2]{0,1:T(2,128)S(1)}, f32[32,2]{0,1:T(2,128)}, u32[]{:S(2)}) copy-start(f32[32,2]{0,1:T(2,128)} %param.45) | copy-start | bytes 772
  0.9 174.3 %copy-start.22 = (f32[2,64]{1,0:T(2,128)S(1)}, f32[2,64]{1,0:T(2,128)}, u32[]{:S(2)}) copy-start(f32[2,64]{1,0:T(2,128)} %refs_24_.1) | copy-start | bytes 1540
  175.0 0.7 copy-start.23
  175.0 0.7 copy-start.24
  175.0 0.7 copy-start.17
  175.7 1.0 copy-start.2
  176.7 0.9 copy-start.10
  177.6 1.8 copy-start.25
  179.3 1.1 copy-start.26
